TPU v7x, 32 devices: a whole 2x2x4 slice. The times are simulated.
32 devices in a mesh: dp: 8 (over z, x), ctx: 4 (over y, core).
Axes of the slice: x: 2, y: 2, z: 4, core: 2. Of those that a mesh axis runs over, the one named last changes fastest.
Arguments:
- tokens: bfloat16 [8, 2048, 768], P('dp', 'ctx'), may hold values from -6 to 6
- doc_ids: int32 [8, 2048], P('dp'), may hold values from 0 to 33, as said below
- pair_table: int32 [4], replicated, may hold values from 0 to 3, each once
- gain_attn: bfloat16 [768], P('dp'), may hold values from 0.5 to 1.5
- gain_ffn: bfloat16 [768], P('dp'), may hold values from 0.5 to 1.5
- w_qkv: bfloat16 [768, 2304], P('dp'), may hold values from -0.21875 to 0.21875
- w_out: bfloat16 [768, 768], P('dp'), may hold values from -2 to 2
- w_in: bfloat16 [768, 2304], P('dp'), may hold values from -0.21875 to 0.21875
- w_down: bfloat16 [1152, 768], P('dp'), may hold values from -0.1875 to 0.1875
- cotangent: bfloat16 [8, 2048, 768], P('dp', 'ctx'), may hold values from -6 to 6
Outputs:
- out_tokens: bfloat16 [8, 2048, 768], P('dp', 'ctx')
- grad_tokens: bfloat16 [8, 2048, 768], P('dp', 'ctx')
- grad_gain_attn: float32 [768], P('dp')
- grad_gain_ffn: float32 [768], P('dp')
- grad_w_qkv: float32 [768, 2304], P('dp')
- grad_w_out: float32 [768, 768], P('dp')
- grad_w_in: float32 [768, 2304], P('dp')
- grad_w_down: float32 [1152, 768], P('dp')
Inputs may be any that keep to these rules, and one draw needn't show every extreme that they name: Along each sequence, in position order, doc_ids start at 0 and rise by 0 or 1 from one position to the next, and the last position of every sequence holds 33; one document of 1025 to 1536 tokens begins or ends each sequence. The device at index j along ctx holds blocks pair_table[j] and 7 - pair_table[j] of each of its sequences.
All inputs are finite; a program needn't handle non-finite values.
Results may differ from a plain program's by a relative error of at most 0.02.
Values may be sent and summed in bfloat16 or wider, within the bound.
A program may use at most 192 MiB of HBM per device.

v0:
```python
import math

import jax
import jax.numpy as jnp
from jax import lax
from jax.sharding import PartitionSpec as P

D = 768
HEADS = 12
HEAD_DIM = 64
FF = 1152


rope_base = 160000.0
norm_eps = 1e-05
masked_score = -1e30


def layer_norm(inputs, scale_gain):
    centre = jnp.mean(inputs, -1, keepdims=True)
    shifted = inputs - centre
    spread = jnp.mean(shifted * shifted, -1, keepdims=True)
    return shifted * lax.rsqrt(spread + norm_eps) * scale_gain


def rotary(inputs, cosine_part, sine_part):
    half_dim = inputs.shape[-1] // 2
    leading = inputs[..., :half_dim]
    trailing = inputs[..., half_dim:]
    return jnp.concatenate(
        [
            leading * cosine_part - trailing * sine_part,
            trailing * cosine_part + leading * sine_part,
        ],
        -1,
    )


def rotary_tables(positions, head_dim):
    exponents = jnp.arange(head_dim // 2, dtype=jnp.float32) * (2.0 / head_dim)
    frequency = jnp.power(jnp.float32(rope_base), -exponents)
    angles = positions.astype(jnp.float32)[:, None] * frequency[None, :]
    return (jnp.cos(angles)[:, None, :], jnp.sin(angles)[:, None, :])


def dealt_positions(pair_table, rows_dev, ctx_size):
    half_rows = rows_dev // 2
    slot_index = jnp.arange(rows_dev * ctx_size, dtype=jnp.int32)
    owner_index = slot_index // rows_dev
    within = slot_index % rows_dev
    leading = jnp.take(pair_table, owner_index)
    block_index = jnp.where(within < half_rows, leading, 2 * ctx_size - 1 - leading)
    return block_index * half_rows + within % half_rows


def gated_gelu(gate_part, up_part):
    return jax.nn.gelu(gate_part, approximate=False) * up_part


def contract_rows(left_side, right_side):
    return lax.dot_general(
        left_side, right_side, (((0,), (0,)), ((), ())), preferred_element_type=jnp.float32
    )


def contract_cols(left_side, right_side):
    return lax.dot_general(
        left_side, right_side, (((1,), (1,)), ((), ())), preferred_element_type=jnp.float32
    )


def allowed_pairs(query_pos, query_doc, key_pos, key_doc):
    return (key_doc[None, :] == query_doc[:, None]) & (key_pos[None, :] <= query_pos[:, None])


def pair_scores(queries, keys):
    return jnp.einsum("qhd,khd->hqk", queries, keys, preferred_element_type=jnp.float32) * (
        1.0 / math.sqrt(HEAD_DIM)
    )


def on_device(
    tokens, doc_ids, pair_table, gain_attn, gain_ffn, w_qkv, w_out, w_in, w_down, cotangent
):
    ctx_size = lax.axis_size("ctx")
    ctx_here = lax.axis_index("ctx")
    rows_dev = tokens.shape[1]
    seq_len = rows_dev * ctx_size
    score_scale = 1.0 / math.sqrt(HEAD_DIM)
    positions = dealt_positions(pair_table, rows_dev, ctx_size)
    doc_slots = jnp.take(doc_ids[0], positions)
    pos_own = lax.dynamic_slice_in_dim(positions, ctx_here * rows_dev, rows_dev)
    doc_own = lax.dynamic_slice_in_dim(doc_slots, ctx_here * rows_dev, rows_dev)
    cosine_part, sine_part = rotary_tables(pos_own, HEAD_DIM)
    attn_scale, ffn_scale, qkv_full, out_full, in_full, down_full = (
        lax.all_gather(gain_attn, "dp", axis=0, tiled=True),
        lax.all_gather(gain_ffn, "dp", axis=0, tiled=True),
        lax.all_gather(w_qkv, "dp", axis=0, tiled=True),
        lax.all_gather(w_out, "dp", axis=0, tiled=True),
        lax.all_gather(w_in, "dp", axis=0, tiled=True),
        lax.all_gather(w_down, "dp", axis=0, tiled=True),
    )
    x_rows = tokens[0].astype(jnp.float32)
    normed_attn, pull_attn = jax.vjp(layer_norm, x_rows, attn_scale.astype(jnp.float32))
    normed_low = normed_attn.astype(jnp.bfloat16)
    qkv_rows = jnp.dot(normed_low, qkv_full, preferred_element_type=jnp.float32)
    shaped = qkv_rows.reshape(rows_dev, 3, HEADS, HEAD_DIM)
    queries = rotary(shaped[:, 0], cosine_part, sine_part).astype(jnp.bfloat16)
    keys_own = rotary(shaped[:, 1], cosine_part, sine_part).astype(jnp.bfloat16)
    values_own = shaped[:, 2].astype(jnp.bfloat16)
    keys_flat, values_flat = (
        lax.all_gather(keys_own.reshape(rows_dev, D), "ctx", axis=0, tiled=True),
        lax.all_gather(values_own.reshape(rows_dev, D), "ctx", axis=0, tiled=True),
    )
    key_rows = min(seq_len, 512)
    key_count = seq_len // key_rows
    block_ids = jnp.arange(key_count, dtype=jnp.int32)

    def fetch_keys(key_table, value_table, block_idx):
        first_row = block_idx * key_rows
        key_part = lax.dynamic_slice_in_dim(key_table, first_row, key_rows).reshape(
            key_rows, HEADS, HEAD_DIM
        )
        value_part = lax.dynamic_slice_in_dim(value_table, first_row, key_rows).reshape(
            key_rows, HEADS, HEAD_DIM
        )
        allowed = allowed_pairs(
            pos_own,
            doc_own,
            lax.dynamic_slice_in_dim(positions, first_row, key_rows),
            lax.dynamic_slice_in_dim(doc_slots, first_row, key_rows),
        )
        return (key_part, value_part, allowed)

    def stats_step(state_pair, block_idx):
        running_top, running_total = state_pair
        key_part, value_part, allowed = fetch_keys(keys_flat, values_flat, block_idx)
        scores = pair_scores(queries, key_part)
        new_top = jnp.maximum(
            running_top, jnp.max(jnp.where(allowed[None], scores, masked_score), -1)
        )
        weights = jnp.where(allowed[None], jnp.exp(scores - new_top[..., None]), 0.0)
        return (
            (new_top, running_total * jnp.exp(running_top - new_top) + jnp.sum(weights, -1)),
            None,
        )

    start_top = jnp.full((HEADS, rows_dev), masked_score, jnp.float32)
    (row_top, row_total), _ = lax.scan(
        stats_step, (start_top, jnp.zeros((HEADS, rows_dev), jnp.float32)), block_ids
    )
    log_total = row_top + jnp.log(row_total)

    def output_step(summed, block_idx):
        key_part, value_part, allowed = fetch_keys(keys_flat, values_flat, block_idx)
        probabilities = jnp.where(
            allowed[None], jnp.exp(pair_scores(queries, key_part) - log_total[..., None]), 0.0
        )
        return (
            summed
            + jnp.einsum(
                "hqk,khd->qhd",
                probabilities.astype(jnp.bfloat16),
                value_part,
                preferred_element_type=jnp.float32,
            ),
            None,
        )

    attended_sum, _ = lax.scan(
        output_step, jnp.zeros((rows_dev, HEADS, HEAD_DIM), jnp.float32), block_ids
    )
    attended = attended_sum.reshape(rows_dev, D).astype(jnp.bfloat16)
    mid_rows = x_rows + jnp.dot(attended, out_full, preferred_element_type=jnp.float32)
    normed_ffn, pull_ffn = jax.vjp(layer_norm, mid_rows, ffn_scale.astype(jnp.float32))
    normed_second = normed_ffn.astype(jnp.bfloat16)
    gate_up = jnp.dot(normed_second, in_full, preferred_element_type=jnp.float32)
    mixed_float, pull_mix = jax.vjp(gated_gelu, gate_up[:, :FF], gate_up[:, FF:])
    mixed_low = mixed_float.astype(jnp.bfloat16)
    out_rows = mid_rows + jnp.dot(mixed_low, down_full, preferred_element_type=jnp.float32)
    d_out_low = cotangent[0]
    grad_down = contract_rows(mixed_low, d_out_low)
    d_mixed = contract_cols(d_out_low, down_full)
    d_gate, d_up = pull_mix(d_mixed)
    d_gate_up = jnp.concatenate([d_gate, d_up], 1).astype(jnp.bfloat16)
    grad_in = contract_rows(normed_second, d_gate_up)
    d_normed_second = contract_cols(d_gate_up, in_full)
    d_mid_norm, grad_ffn_gain = pull_ffn(d_normed_second)
    d_mid = d_out_low.astype(jnp.float32) + d_mid_norm
    d_branch = d_mid.astype(jnp.bfloat16)
    grad_out = contract_rows(attended, d_branch)
    d_att = (
        contract_cols(d_branch, out_full).astype(jnp.bfloat16).reshape(rows_dev, HEADS, HEAD_DIM)
    )
    row_delta = jnp.transpose(jnp.sum(d_att.astype(jnp.float32) * attended_sum, -1))
    keys_back, values_back = (
        lax.all_gather(keys_own.reshape(rows_dev, D), "ctx", axis=0, tiled=True),
        lax.all_gather(values_own.reshape(rows_dev, D), "ctx", axis=0, tiled=True),
    )

    def grad_step(d_query_sum, block_idx):
        key_part, value_part, allowed = fetch_keys(keys_back, values_back, block_idx)
        probabilities = jnp.where(
            allowed[None], jnp.exp(pair_scores(queries, key_part) - log_total[..., None]), 0.0
        )
        d_probs = jnp.einsum("qhd,khd->hqk", d_att, value_part, preferred_element_type=jnp.float32)
        d_scores = (probabilities * (d_probs - row_delta[..., None])).astype(jnp.bfloat16)
        d_query_sum = (
            d_query_sum
            + jnp.einsum("hqk,khd->qhd", d_scores, key_part, preferred_element_type=jnp.float32)
            * score_scale
        )
        d_key_part = (
            jnp.einsum("hqk,qhd->khd", d_scores, queries, preferred_element_type=jnp.float32)
            * score_scale
        )
        d_value_part = jnp.einsum(
            "hqk,qhd->khd",
            probabilities.astype(jnp.bfloat16),
            d_att,
            preferred_element_type=jnp.float32,
        )
        return (d_query_sum, (d_key_part.reshape(key_rows, D), d_value_part.reshape(key_rows, D)))

    d_queries, (d_keys_all, d_values_all) = lax.scan(
        grad_step, jnp.zeros((rows_dev, HEADS, HEAD_DIM), jnp.float32), block_ids
    )
    d_keys, d_values = (
        lax.psum_scatter(
            d_keys_all.reshape(seq_len, D).astype(jnp.bfloat16),
            "ctx",
            scatter_dimension=0,
            tiled=True,
        ).astype(jnp.float32),
        lax.psum_scatter(
            d_values_all.reshape(seq_len, D).astype(jnp.bfloat16),
            "ctx",
            scatter_dimension=0,
            tiled=True,
        ).astype(jnp.float32),
    )
    negative_sine = -sine_part
    d_qkv = jnp.concatenate(
        [
            rotary(d_queries, cosine_part, negative_sine).reshape(rows_dev, D),
            rotary(d_keys.reshape(rows_dev, HEADS, HEAD_DIM), cosine_part, negative_sine).reshape(
                rows_dev, D
            ),
            d_values,
        ],
        1,
    ).astype(jnp.bfloat16)
    grad_qkv = contract_rows(normed_low, d_qkv)
    d_normed_attn = contract_cols(d_qkv, qkv_full)
    d_x_norm, grad_attn_gain = pull_attn(d_normed_attn)
    grad_rows = (d_mid + d_x_norm).astype(jnp.bfloat16)
    owned = (
        lax.psum_scatter(
            grad_attn_gain.astype(jnp.bfloat16), "dp", scatter_dimension=0, tiled=True
        ).astype(jnp.float32),
        lax.psum_scatter(
            grad_ffn_gain.astype(jnp.bfloat16), "dp", scatter_dimension=0, tiled=True
        ).astype(jnp.float32),
        lax.psum_scatter(
            grad_qkv.astype(jnp.bfloat16), "dp", scatter_dimension=0, tiled=True
        ).astype(jnp.float32),
        lax.psum_scatter(
            grad_out.astype(jnp.bfloat16), "dp", scatter_dimension=0, tiled=True
        ).astype(jnp.float32),
        lax.psum_scatter(
            grad_in.astype(jnp.bfloat16), "dp", scatter_dimension=0, tiled=True
        ).astype(jnp.float32),
        lax.psum_scatter(
            grad_down.astype(jnp.bfloat16), "dp", scatter_dimension=0, tiled=True
        ).astype(jnp.float32),
    )
    owned_attn, owned_ffn, owned_qkv, owned_out, owned_in, owned_down = owned
    summed_attn, summed_ffn, summed_qkv, summed_out, summed_in, summed_down = (
        lax.psum(owned_attn.astype(jnp.bfloat16), "ctx").astype(jnp.float32),
        lax.psum(owned_ffn.astype(jnp.bfloat16), "ctx").astype(jnp.float32),
        lax.psum(owned_qkv.astype(jnp.bfloat16), "ctx").astype(jnp.float32),
        lax.psum(owned_out.astype(jnp.bfloat16), "ctx").astype(jnp.float32),
        lax.psum(owned_in.astype(jnp.bfloat16), "ctx").astype(jnp.float32),
        lax.psum(owned_down.astype(jnp.bfloat16), "ctx").astype(jnp.float32),
    )
    return (
        out_rows.astype(jnp.bfloat16)[None],
        grad_rows[None],
        summed_attn,
        summed_ffn,
        summed_qkv,
        summed_out,
        summed_in,
        summed_down,
    )


def solution(mesh):
    return jax.shard_map(
        on_device,
        mesh=mesh,
        in_specs=(
            P("dp", "ctx", None),
            P("dp", None),
            P(),
            P("dp"),
            P("dp"),
            P("dp", None),
            P("dp", None),
            P("dp", None),
            P("dp", None),
            P("dp", "ctx", None),
        ),
        out_specs=(
            P("dp", "ctx", None),
            P("dp", "ctx", None),
            P("dp"),
            P("dp"),
            P("dp", None),
            P("dp", None),
            P("dp", None),
            P("dp", None),
        ),
        check_vma=False,
    )
```

profile of v0, /device:TPU:0, one launch (start us, length us, event | category | flops | bytes accessed | tf_op | source)
XLA Modules:
  0.0 904.1 jit_solution(1952635748762256828)
XLA Ops:
  11.6 23.2 %all-reduce.5 = (bf16[768]{0:T(1024)(128)(2,1)S(1)}, bf16[768]{0:T(1024)(128)(2,1)S(1)}) all-reduce(bf16[768]{0:T(1024)(128)(2,1)S(1)} %dynamic-update-slice, bf16[768]{0:T(1024)(128)(2,1)S(1)} %dynamic-update-slice.1), channel_id=1, replica_groups=mesh['dp'=8,'ctx'=4] {'dp'}, use_global_device_ids=true, to_apply=%add | all-reduce | flops 1536 | bytes 6144
  38.9 11.8 %gather_fusion = s32[2048]{0:T(1024)S(1)} fusion(s32[2048]{0:T(1024)S(1)} %bitcast.217, s32[2048]{0:T(1024)S(1)} %broadcast_clamp_fusion), kind=kCustom, calls=%fused_computation | custom fusion | bytes 24576 | tf_op jit(solution)/shard_map/jit(_take)/gather | solution.py:91
  52.4 25.9 %all-gather.7.cloned.1.call-done = bf16[768,2304]{1,0:T(8,128)(2,1)} async-done(((bf16[96,2304]{1,0:T(8,128)(2,1)}), bf16[768,2304]{1,0:T(8,128)(2,1)}) %all-gather.7.cloned.1.call-update) | async-done | bytes 3538960 | tf_op jit(solution)/shard_map/all_gather | solution.py:98
  78.3 5.8 copy.41
  84.1 4.2 fusion.50
  96.7 22.5 %all-gather.11.cloned.1.call-done = bf16[2048,768]{0,1:T(8,128)(2,1)} async-done(((bf16[512,768]{0,1:T(8,128)(2,1)}), bf16[2048,768]{0,1:T(8,128)(2,1)}) %all-gather.11.cloned.1.call-update) | async-done | bytes 3145744 | tf_op jit(solution)/shard_map/all_gather | solution.py:112
  119.2 30.5 %while.39 = (s32[]{:T(128)}, f32[12,512]{1,0:T(8,128)S(1)}, f32[12,512]{1,0:T(8,128)S(1)}, s32[4]{0:T(128)S(1)}, s32[2048]{0:T(1024)S(1)}, /*index=5*/s32[512]{0...) while((s32[]{:T(128)}, f32[12,512]{1,0:T(8,128)S(1)}, ...), condition=%wide.region_5.6_spmd.clone, body=%wide.region_2.5_spmd.clone.sunk | while | flops 425490432 | bytes 29434076 | solution.py:149
  149.9 36.2 %while.40 = (s32[]{:T(128)}, f32[512,12,64]{0,2,1:T(8,128)}, s32[4]{0:T(128)S(1)}, bf16[2048,768]{0,1:T(8,128)(2,1)}, s32[2048]{0:T(1024)S(1)}, /*index=5*/s32[5...) while((s32[]{:T(128)}, f32[512,12,64]{0,2,1:T(8,128)}, ...), condition=%wide.region_7.8_spmd.clone, body=%wide.region_6.7_spmd.clone.sunk | while | flops 819462144 | bytes 9216229 | solution.py:170
  153.1 4.8 bitcast_add_fusion.4
  161.1 6.2 bitcast_add_fusion.4
  170.5 6.2 bitcast_add_fusion.4
  179.8 6.2 bitcast_add_fusion.4
  188.5 4.5 all-gather.13.cloned.1.call-done
  195.8 63.3 %all-gather.15.cloned.1.call-done = bf16[768,2304]{1,0:T(8,128)(2,1)} async-done(((bf16[96,2304]{1,0:T(8,128)(2,1)}), bf16[768,2304]{1,0:T(8,128)(2,1)}) %all-gather.15.cloned.1.call-update) | async-done | bytes 3538960 | tf_op jit(solution)/shard_map/all_gather | solution.py:100
  259.0 6.3 fusion.84
  265.3 40.2 %all-gather.17.cloned.1.call-done = bf16[1152,768]{1,0:T(8,128)(2,1)} async-done(((bf16[144,768]{1,0:T(8,128)(2,1)}), bf16[1152,768]{1,0:T(8,128)(2,1)}) %all-gather.17.cloned.1.call-update) | async-done | bytes 1769488 | tf_op jit(solution)/shard_map/all_gather | solution.py:101
  305.5 9.1 %add_convert_fusion = (bf16[512,1152]{1,0:T(8,128)(2,1)S(1)}, f32[512,1152]{1,0:T(8,128)S(1)}, f32[512,1152]{1,0:T(8,128)S(1)}) fusion(f32[512,2304]{1,0:T(8,128)} %fusion.84, bf16[1152,768]{1,0:T(8,128)(2,1)} %all-gather.17.cloned.1.call-done, bf16[1,512,768]{2,1,0:T(8,128)(2,1)S(1)} %copy-done.17), kind=kOutput, calls=%fused_computation.51 | convolution fusion | flops 949026816 | bytes 13172736 | tf_op jit(solution)/shard_map/dot_general | solution.py:67
  327.2 144.4 %while.41 = (s32[]{:T(128)}, f32[512,12,64]{0,2,1:T(8,128)}, bf16[4,512,768]{2,1,0:T(8,128)(2,1)}, bf16[4,512,768]{2,1,0:T(8,128)(2,1)}, s32[4]{0:T(128)S(1)}, /...) while((s32[]{:T(128)}, f32[512,12,64]{0,2,1:T(8,128)}, ...), condition=%wide.region_14.15_spmd.clone, body=%wide.region_13.14_spmd.clone.sunk | while | flops 2047475712 | bytes 105472392 | solution.py:225
  336.3 4.6 fusion.164
  340.9 8.4 fusion.163
  350.9 5.5 bitcast_add_fusion.5
  356.4 4.0 convolution_multiply_fusion.2
  372.1 4.6 fusion.164
  376.6 8.4 fusion.163
  386.6 5.9 bitcast_add_fusion.5
  392.5 4.0 convolution_multiply_fusion.2
  408.2 4.6 fusion.164
  412.8 8.4 fusion.163
  422.8 5.9 bitcast_add_fusion.5
  428.7 4.0 convolution_multiply_fusion.2
  444.4 4.6 fusion.164
  448.9 8.4 fusion.163
  458.9 5.9 bitcast_add_fusion.5
  464.8 4.0 convolution_multiply_fusion.2
  477.6 6.2 convolution_convert_fusion
  483.8 24.9 %reduce-scatter.7.cloned.1.call-done = bf16[512,768]{1,0:T(8,128)(2,1)} async-done(((bf16[2048,768]{1,0:T(8,128)(2,1)}), bf16[512,768]{1,0:T(8,128)(2,1)}) %reduce-scatter.7.cloned.1.call-update) | async-done | bytes 786448 | tf_op jit(solution)/shard_map/reduce_scatter | solution.py:229
  513.7 35.7 %reduce-scatter.9.cloned.1.call-done = bf16[512,768]{1,0:T(8,128)(2,1)} async-done(((bf16[2048,768]{1,0:T(8,128)(2,1)}), bf16[512,768]{1,0:T(8,128)(2,1)}) %reduce-scatter.9.cloned.1.call-update) | async-done | bytes 786448 | tf_op jit(solution)/shard_map/reduce_scatter | solution.py:235
  549.5 5.3 convolution_convert_fusion.1
  556.5 3.7 fusion.45
  560.2 3.2 fusion.40
  563.5 53.4 %reduce-scatter.13.cloned.1.call-done = bf16[96,768]{1,0:T(8,128)(2,1)} async-done(((bf16[768,768]{1,0:T(8,128)(2,1)}), bf16[96,768]{1,0:T(8,128)(2,1)}) %reduce-scatter.13.cloned.1.call-update) | async-done | bytes 147472 | tf_op jit(solution)/shard_map/reduce_scatter | solution.py:267
  616.9 68.2 %reduce-scatter.17.cloned.1.call-done = bf16[144,768]{1,0:T(8,128)(2,1)} async-done(((bf16[1152,768]{1,0:T(8,128)(2,1)}), bf16[144,768]{1,0:T(8,128)(2,1)}) %reduce-scatter.17.cloned.1.call-update) | async-done | bytes 221200 | tf_op jit(solution)/shard_map/reduce_scatter | solution.py:273
  685.0 82.0 %reduce-scatter.15.cloned.1.call-done = bf16[96,2304]{1,0:T(8,128)(2,1)} async-done(((bf16[768,2304]{1,0:T(8,128)(2,1)}), bf16[96,2304]{1,0:T(8,128)(2,1)}) %reduce-scatter.15.cloned.1.call-update) | async-done | bytes 442384 | tf_op jit(solution)/shard_map/reduce_scatter | solution.py:270
  767.0 82.6 %reduce-scatter.11.cloned.1.call-done = bf16[96,2304]{1,0:T(8,128)(2,1)} async-done(((bf16[768,2304]{1,0:T(8,128)(2,1)}), bf16[96,2304]{1,0:T(8,128)(2,1)}) %reduce-scatter.11.cloned.1.call-update) | async-done | bytes 442384 | tf_op jit(solution)/shard_map/reduce_scatter | solution.py:264
  851.9 20.0 %all-reduce.4 = (bf16[768]{0:T(1024)(128)(2,1)S(1)}, bf16[768]{0:T(1024)(128)(2,1)S(1)}) all-reduce(bf16[768]{0:T(1024)(128)(2,1)S(1)} %get-tuple-element.359, bf16[768]{0:T(1024)(128)(2,1)S(1)} %copy-done.46), channel_id=4, replica_groups=mesh['dp'=8,'ctx'=4] {'dp'}, use_global_device_ids=true, to_apply=%region_20.21.clone | all-reduce | flops 1536 | bytes 6144
  872.0 5.6 all-reduce.6
  878.7 3.1 fusion.48
  881.7 9.2 %all-reduce.10.cloned.1.call-done = (bf16[96,2304]{1,0:T(8,128)(2,1)}, bf16[96,768]{1,0:T(8,128)(2,1)}, bf16[96,2304]{1,0:T(8,128)(2,1)}, bf16[144,768]{1,0:T(8,128)(2,1)}) async-done(((bf16[96,2304]{1,0:T(8,128)(2,1)}, bf16[96,768]{1,0:T(8,128)(2,1)}, bf16[96,2304]{1,0:T(8,128)(2,1)}, bf16[144,768]{1,0:T(8,128)(2,1)}), (bf16[96,2304]{1,0:T(8,128)(2,1)}, bf16[96,768]{1,0:T(8,128)(2,1)}, ...) | async-done | bytes 1253392 | tf_op jit(solution)/shard_map/psum | solution.py:281
  (334 shorter events, 144.9 us)
Async XLA Ops:
  7.2 31.7 %copy-start = (s32[1,2048]{1,0:T(1,128)S(1)}, s32[1,2048]{1,0:T(1,128)}, u32[]{:S(2)}) copy-start(s32[1,2048]{1,0:T(1,128)} %param.17) | copy-start | bytes 24580
  7.2 71.1 %all-gather.7.cloned.1.call-start = ((), (), s32[]{:S(2)}) async-start(), calls=%async_computation.6 | async-start | bytes 3981312 | tf_op jit(solution)/shard_map/all_gather | solution.py:98
  7.9 111.3 %all-gather.11.cloned.1.call-start = ((), (), s32[]{:S(2)}) async-start(), calls=%async_computation.8 | async-start | bytes 3932160 | tf_op jit(solution)/shard_map/all_gather | solution.py:112
  34.9 49.2 %copy-start.33 = (f32[768]{0:T(1024)}, f32[768]{0:T(1024)S(1)}, u32[]{:S(2)}) copy-start(f32[768]{0:T(1024)S(1)} %convert_element_type.140) | copy-start | bytes 9220
  38.9 11.9 %copy-start.8 = (bf16[1,512,768]{2,1,0:T(8,128)(2,1)S(1)}, bf16[1,512,768]{2,1,0:T(8,128)(2,1)}, u32[]{:S(2)}) copy-start(bf16[1,512,768]{2,1,0:T(8,128)(2,1)} %param.16) | copy-start | bytes 2359300
  51.0 33.1 %copy-start.35 = (f32[512]{0:T(512)}, f32[512]{0:T(512)S(1)}, u32[]{:S(2)}) copy-start(f32[512]{0:T(512)S(1)} %broadcast_multiply_fusion.1) | copy-start | bytes 6148
  51.4 32.7 %copy-start.37 = (f32[512]{0:T(512)}, f32[512]{0:T(512)S(1)}, u32[]{:S(2)}) copy-start(f32[512]{0:T(512)S(1)} %fusion.39) | copy-start | bytes 6148
  51.4 32.7 %copy-start.39 = (f32[512]{0:T(512)}, f32[512]{0:T(512)S(1)}, u32[]{:S(2)}) copy-start(f32[512]{0:T(512)S(1)} %fusion.77) | copy-start | bytes 6148
  52.4 38.1 %copy-start.31 = (f32[512,32]{0,1:T(8,128)}, f32[512,32]{0,1:T(8,128)S(1)}, u32[]{:S(2)}) copy-start(f32[512,32]{0,1:T(8,128)S(1)} %get-tuple-element.475) | copy-start | bytes 196612
  92.0 57.9 %all-gather.9.cloned.1.call-start = ((), (), s32[]{:S(2)}) async-start(), calls=%async_computation.7 | async-start | bytes 3932160 | tf_op jit(solution)/shard_map/all_gather | solution.py:113
  94.4 98.6 %all-gather.13.cloned.1.call-start = ((), (), s32[]{:S(2)}) async-start(), calls=%async_computation.9 | async-start | bytes 1327104 | tf_op jit(solution)/shard_map/all_gather | solution.py:99
  95.0 164.0 %all-gather.15.cloned.1.call-start = ((), (), s32[]{:S(2)}) async-start(), calls=%async_computation.10 | async-start | bytes 3981312 | tf_op jit(solution)/shard_map/all_gather | solution.py:100
  95.6 209.9 %all-gather.17.cloned.1.call-start = ((), (), s32[]{:S(2)}) async-start(), calls=%async_computation.11 | async-start | bytes 1990656 | tf_op jit(solution)/shard_map/all_gather | solution.py:101
  96.2 412.6 %reduce-scatter.7.cloned.1.call-start = ((), (), s32[]{:S(2)}) async-start(), calls=%async_computation.12 | async-start | bytes 3932160 | tf_op jit(solution)/shard_map/reduce_scatter | solution.py:229
  195.4 125.3 %copy-start.11 = (f32[512,768]{1,0:T(8,128)}, f32[512,768]{1,0:T(8,128)S(1)}, u32[]{:S(2)}) copy-start(f32[512,768]{1,0:T(8,128)S(1)} %get-tuple-element.483) | copy-start | bytes 4718596
  195.8 125.0 %copy-start.44 = (f32[512]{0:T(512)}, f32[512]{0:T(512)S(1)}, u32[]{:S(2)}) copy-start(f32[512]{0:T(512)S(1)} %fusion.78) | copy-start | bytes 6148
  195.8 109.8 %copy-start.17 = (bf16[1,512,768]{2,1,0:T(8,128)(2,1)S(1)}, bf16[1,512,768]{2,1,0:T(8,128)(2,1)}, u32[]{:S(2)}) copy-start(bf16[1,512,768]{2,1,0:T(8,128)(2,1)} %param.25) | copy-start | bytes 2359300
  305.5 9.1 %copy-start.14 = (f32[512,2304]{1,0:T(8,128)S(1)}, f32[512,2304]{1,0:T(8,128)}, u32[]{:S(2)}) copy-start(f32[512,2304]{1,0:T(8,128)} %fusion.84) | copy-start | bytes 14155780
  327.4 5.1 copy-start.3
  349.4 7.0 slice-start
  350.9 5.5 slice-start.1
  385.1 7.4 slice-start
  386.6 5.9 slice-start.1
  399.3 5.0 copy-start.3
  421.2 7.4 slice-start
  422.8 5.9 slice-start.1
  457.4 7.4 slice-start
  458.9 5.9 slice-start.1
  471.7 77.8 %reduce-scatter.9.cloned.1.call-start = ((), (), s32[]{:S(2)}) async-start(), calls=%async_computation.13 | async-start | bytes 3932160 | tf_op jit(solution)/shard_map/reduce_scatter | solution.py:235
  472.4 144.4 %reduce-scatter.13.cloned.1.call-start = ((), (), s32[]{:S(2)}) async-start(), calls=%async_computation.15 | async-start | bytes 1327104 | tf_op jit(solution)/shard_map/reduce_scatter | solution.py:267
  474.8 210.2 %reduce-scatter.17.cloned.1.call-start = ((), (), s32[]{:S(2)}) async-start(), calls=%async_computation.17 | async-start | bytes 1990656 | tf_op jit(solution)/shard_map/reduce_scatter | solution.py:273
  477.3 289.7 %reduce-scatter.15.cloned.1.call-start = ((), (), s32[]{:S(2)}) async-start(), calls=%async_computation.16 | async-start | bytes 3981312 | tf_op jit(solution)/shard_map/reduce_scatter | solution.py:270
  483.8 26.4 %copy-start.5 = (f32[512,12,64]{0,2,1:T(8,128)S(1)}, f32[512,12,64]{0,2,1:T(8,128)}, u32[]{:S(2)}) copy-start(f32[512,12,64]{0,2,1:T(8,128)} %get-tuple-element.200) | copy-start | bytes 4718596
  483.8 365.8 %reduce-scatter.11.cloned.1.call-start = ((), (), s32[]{:S(2)}) async-start(), calls=%async_computation.14 | async-start | bytes 3981312 | tf_op jit(solution)/shard_map/reduce_scatter | solution.py:264
  512.4 37.0 %copy-start.9 = (bf16[1,512,768]{2,1,0:T(8,128)(2,1)S(1)}, bf16[1,512,768]{2,1,0:T(8,128)(2,1)}, u32[]{:S(2)}) copy-start(bf16[1,512,768]{2,1,0:T(8,128)(2,1)} %param.16) | copy-start | bytes 2359300
  512.4 37.0 %copy-start.34 = (f32[768]{0:T(1024)S(1)}, f32[768]{0:T(1024)}, u32[]{:S(2)}) copy-start(f32[768]{0:T(1024)} %copy-done.33) | copy-start | bytes 9220
  512.5 37.0 %copy-start.36 = (f32[512]{0:T(512)S(1)}, f32[512]{0:T(512)}, u32[]{:S(2)}) copy-start(f32[512]{0:T(512)} %copy-done.35) | copy-start | bytes 6148
  512.5 37.0 %copy-start.40 = (f32[512]{0:T(512)S(1)}, f32[512]{0:T(512)}, u32[]{:S(2)}) copy-start(f32[512]{0:T(512)} %copy-done.39) | copy-start | bytes 6148
  512.8 36.7 %copy-start.24 = (bf16[512,768]{1,0:T(8,128)(2,1)}, bf16[512,768]{1,0:T(8,128)(2,1)S(1)}, u32[]{:S(2)}) copy-start(bf16[512,768]{1,0:T(8,128)(2,1)S(1)} %copy.46) | copy-start | bytes 2359300
  513.7 35.8 %copy-start.26 = (bf16[512,768]{1,0:T(8,128)(2,1)}, bf16[512,768]{1,0:T(8,128)(2,1)S(1)}, u32[]{:S(2)}) copy-start(bf16[512,768]{1,0:T(8,128)(2,1)S(1)} %copy.47) | copy-start | bytes 2359300
  554.7 336.2 %all-reduce.10.cloned.1.call-start = ((), (), s32[]{:S(2)}) async-start(), calls=%async_computation.18 | async-start | bytes 2506752 | tf_op jit(solution)/shard_map/psum | solution.py:281
  563.5 288.4 %copy-start.46 = (bf16[768]{0:T(1024)(128)(2,1)S(1)}, bf16[768]{0:T(1024)(128)(2,1)}, u32[]{:S(2)}) copy-start(bf16[768]{0:T(1024)(128)(2,1)} %get-tuple-element.357) | copy-start | bytes 4612
  563.5 315.2 %copy-start.7 = (f32[512,768]{1,0:T(8,128)S(1)}, f32[512,768]{1,0:T(8,128)}, u32[]{:S(2)}) copy-start(f32[512,768]{1,0:T(8,128)} %copy-done.6) | copy-start | bytes 4718596
  563.5 315.2 %copy-start.19 = (bf16[1,512,768]{2,1,0:T(8,128)(2,1)S(1)}, bf16[1,512,768]{2,1,0:T(8,128)(2,1)}, u32[]{:S(2)}) copy-start(bf16[1,512,768]{2,1,0:T(8,128)(2,1)} %param.25) | copy-start | bytes 2359300
  563.5 315.2 %copy-start.41 = (f32[512]{0:T(512)S(1)}, f32[512]{0:T(512)}, u32[]{:S(2)}) copy-start(f32[512]{0:T(512)} %copy-done.39) | copy-start | bytes 6148
  563.5 315.2 %copy-start.43 = (f32[512]{0:T(512)S(1)}, f32[512]{0:T(512)}, u32[]{:S(2)}) copy-start(f32[512]{0:T(512)} %copy-done.42) | copy-start | bytes 6148
  878.7 18.7 %copy-start.1 = (s32[1,2048]{1,0:T(1,128)S(1)}, s32[1,2048]{1,0:T(1,128)}, u32[]{:S(2)}) copy-start(s32[1,2048]{1,0:T(1,128)} %param.17) | copy-start | bytes 24580
  891.0 5.4 copy-start.32
  (33 other events, 81.1 us)
Sparse Core Ops, SparseCore 0:
  10.2 68.0 all-gather.6
  92.1 27.0 all-gather.10
  121.3 28.5 all-gather.8
  151.9 41.0 all-gather.12
  195.0 63.9 all-gather.14
  261.1 44.4 all-gather.16
  471.8 36.9 reduce-scatter.6
  511.4 37.9 reduce-scatter.8
  552.8 64.0 reduce-scatter.12
  620.2 64.8 reduce-scatter.16
  689.1 77.8 reduce-scatter.14
  770.9 78.6 reduce-scatter.10
  852.4 38.4 all-reduce.9
where the time goes:
time: 911 us; the launch traced here: 904 us
  waiting for transfers between devices  516 us (57%)
  matrix products  183 us (20%)
  local copies, waits for them, and re-layouts  89.7 us (10%)
  blocking collectives  48.8 us (5%)
  other arithmetic  41.1 us (5%)
  between operations  16.3 us (2%)
    reduce_scatter x1, waiting for transfers between devices, on_device(): lax.psum_scatter(grad_qkv.astype(jnp.bfloat16), 'dp', scatter_dimension=0...  82.6 us
    reduce_scatter x1, waiting for transfers between devices, on_device(): lax.psum_scatter(grad_in.astype(jnp.bfloat16), 'dp', scatter_dimension=0,...  82 us
    reduce_scatter x1, waiting for transfers between devices, on_device(): lax.psum_scatter(grad_down.astype(jnp.bfloat16), 'dp', scatter_dimension=...  68.2 us
    all_gather x1, waiting for transfers between devices, on_device(): lax.all_gather(w_in, 'dp', axis=0, tiled=True)  63.3 us
    reduce_scatter x1, waiting for transfers between devices, on_device(): lax.psum_scatter(grad_out.astype(jnp.bfloat16), 'dp', scatter_dimension=0...  53.4 us
    unnamed x2, blocking collectives  43.2 us
    all_gather x1, waiting for transfers between devices, on_device(): lax.all_gather(w_down, 'dp', axis=0, tiled=True)  40.2 us
    reduce_scatter x1, waiting for transfers between devices, on_device(): lax.psum_scatter(d_values_all.reshape(seq_len, D).astype(jnp.bfloat16), '...  35.7 us
  transfers between devices with their start and end apart: 13, of which 13 were waited for; matrix products, arithmetic and copies ran while one was open for 14% of the time, Pallas kernels for 0%

commit v1 on v0

v1 whole, which is shorter than its diff:
```python
import math

import jax
import jax.numpy as jnp
from jax import lax
from jax.experimental import pallas as pl
from jax.experimental.pallas import tpu as pltpu
from jax.sharding import PartitionSpec as P

D = 768
HEADS = 12
HEAD_DIM = 64
FF = 1152
PAIRS = HEADS // 2
WIDE = 2 * HEAD_DIM

rope_base = 160000.0
norm_eps = 1e-05
masked_score = -1e30
score_scale = 1.0 / math.sqrt(HEAD_DIM)
vmem_bytes = 56 * 2**20


def contract(left, right, left_dim, right_dim):
    return lax.dot_general(
        left, right, (((left_dim,), (right_dim,)), ((), ())), preferred_element_type=jnp.float32
    )


def fill_bias(bias_ref, qpos_ref, qdoc_ref, kpos_ref, kdoc_ref, sub):
    def fill(block, carry):
        rows = pl.ds(pl.multiple_of(block * sub, sub), sub)
        ok = (kdoc_ref[rows, :] == qdoc_ref[...]) & (kpos_ref[rows, :] <= qpos_ref[...])
        bias_ref[rows, :] = jnp.where(ok, 0.0, masked_score)
        return carry

    lax.fori_loop(0, bias_ref.shape[0] // sub, fill, 0)


def both_heads(block):
    lane = lax.broadcasted_iota(jnp.int32, block.shape, 1)
    wide = block.astype(jnp.float32)
    return jnp.concatenate(
        [jnp.where(lane < HEAD_DIM, wide, 0.0), jnp.where(lane < HEAD_DIM, 0.0, wide)], 0
    ).astype(jnp.bfloat16)


def attend_kernel(
    seen_ref, q_ref, k_ref, v_ref, qpos_ref, qdoc_ref, kpos_ref, kdoc_ref,
    att_ref, lse_ref, bias_ref, top_ref, total_ref, acc_ref,
):
    sub = q_ref.shape[0] // 2
    blocks = k_ref.shape[0] // sub

    @pl.when(pl.program_id(0) == 0)
    def _():
        fill_bias(bias_ref, qpos_ref, qdoc_ref, kpos_ref, kdoc_ref, sub)

    for qb in range(2):
        own = slice(qb * sub, (qb + 1) * sub)
        queries = both_heads(q_ref[own, :])
        top_ref[...] = jnp.full(top_ref.shape, masked_score, jnp.float32)
        total_ref[...] = jnp.zeros(total_ref.shape, jnp.float32)
        acc_ref[...] = jnp.zeros(acc_ref.shape, jnp.float32)

        def step(kb, carry):
            @pl.when(seen_ref[qb * blocks + kb] != 0)
            def _():
                rows = pl.ds(pl.multiple_of(kb * sub, sub), sub)
                bias = bias_ref[rows, own]
                scores = contract(k_ref[rows, :], queries, 1, 1) + jnp.concatenate([bias, bias], 1)
                top = top_ref[...]
                new_top = jnp.maximum(top, jnp.max(scores, 0, keepdims=True))
                shrink = jnp.exp(top - new_top)
                weights = jnp.exp(scores - new_top)
                top_ref[...] = new_top
                total_ref[...] = total_ref[...] * shrink + jnp.sum(weights, 0, keepdims=True)
                acc_ref[...] = acc_ref[...] * shrink + contract(
                    v_ref[rows, :], weights.astype(jnp.bfloat16), 0, 0
                )

            return carry

        lax.fori_loop(0, blocks, step, 0)
        total = total_ref[...]
        scaled = acc_ref[...] / total
        turned = jnp.concatenate([scaled[:HEAD_DIM, :sub], scaled[HEAD_DIM:, sub:]], 0)
        att_ref[own, :] = turned.T
        lse_ref[0, qb : qb + 1, :] = top_ref[...] + jnp.log(total)


def pull_kernel(
    seen_ref, q_ref, k_ref, v_ref, datt_ref, att_ref, lse_ref,
    qpos_ref, qdoc_ref, kpos_ref, kdoc_ref,
    dq_ref, dkv_ref,
    bias_ref, queries_ref, datts_ref, delta_ref, dq_acc, dk_acc, dv_acc,
):
    sub = q_ref.shape[0] // 2
    blocks = k_ref.shape[0] // sub

    @pl.when(pl.program_id(0) == 0)
    def _():
        fill_bias(bias_ref, qpos_ref, qdoc_ref, kpos_ref, kdoc_ref, sub)

    for qb in range(2):
        own = slice(qb * sub, (qb + 1) * sub)
        queries_ref[qb] = both_heads(q_ref[own, :])
        datts_ref[qb] = both_heads(datt_ref[own, :])
        product = (datt_ref[own, :].astype(jnp.float32) * att_ref[own, :]).T
        delta_ref[qb : qb + 1, :] = jnp.concatenate(
            [
                jnp.sum(product[:HEAD_DIM], 0, keepdims=True),
                jnp.sum(product[HEAD_DIM:], 0, keepdims=True),
            ],
            1,
        )
    dq_acc[...] = jnp.zeros(dq_acc.shape, jnp.float32)

    def step(kb, carry):
        rows = pl.ds(pl.multiple_of(kb * sub, sub), sub)
        dk_acc[...] = jnp.zeros(dk_acc.shape, jnp.float32)
        dv_acc[...] = jnp.zeros(dv_acc.shape, jnp.float32)
        for qb in range(2):
            own = slice(qb * sub, (qb + 1) * sub)

            @pl.when(seen_ref[qb * blocks + kb] != 0)
            def _():
                keys = k_ref[rows, :]
                bias = bias_ref[rows, own]
                queries = queries_ref[qb]
                datts = datts_ref[qb]
                scores = contract(keys, queries, 1, 1) + jnp.concatenate([bias, bias], 1)
                weights = jnp.exp(scores - lse_ref[0, qb : qb + 1, :])
                d_weights = contract(v_ref[rows, :], datts, 1, 1)
                d_scores = (weights * (d_weights - delta_ref[qb : qb + 1, :])).astype(jnp.bfloat16)
                dv_acc[...] += contract(weights.astype(jnp.bfloat16), datts, 1, 0)
                dk_acc[...] += contract(d_scores, queries, 1, 0)
                dq_acc[qb] += contract(d_scores, keys, 0, 0)

        dkv_ref[0, rows, :] = dk_acc[...].astype(jnp.bfloat16)
        dkv_ref[1, rows, :] = dv_acc[...].astype(jnp.bfloat16)
        return carry

    lax.fori_loop(0, blocks, step, 0)
    lane = lax.broadcasted_iota(jnp.int32, (sub, WIDE), 1)
    for qb in range(2):
        own = slice(qb * sub, (qb + 1) * sub)
        dq_ref[own, :] = (
            jnp.where(lane < HEAD_DIM, dq_acc[qb, :sub, :], dq_acc[qb, sub:, :]) * score_scale
        )


def whole(shape):
    return pl.BlockSpec(shape, lambda pair: tuple(0 for _ in shape))


def per_pair(rows, first=0):
    return pl.BlockSpec((rows, WIDE), lambda pair: (0, first + pair))


def attend(seen, queries, kv, marks):
    rows, length = queries.shape[0], kv.shape[0]
    sub = rows // 2
    pairs = queries.shape[1] // WIDE
    return pl.pallas_call(
        attend_kernel,
        grid=(pairs,),
        in_specs=[
            pl.BlockSpec(memory_space=pltpu.SMEM),
            per_pair(rows), per_pair(length), per_pair(length, PAIRS),
            whole((1, rows)), whole((1, rows)), whole((length, 1)), whole((length, 1)),
        ],
        out_specs=[per_pair(rows), pl.BlockSpec((1, 2, rows), lambda pair: (pair, 0, 0))],
        out_shape=[
            jax.ShapeDtypeStruct((rows, queries.shape[1]), jnp.float32),
            jax.ShapeDtypeStruct((pairs, 2, rows), jnp.float32),
        ],
        scratch_shapes=[
            pltpu.VMEM((length, rows), jnp.float32),
            pltpu.VMEM((1, rows), jnp.float32),
            pltpu.VMEM((1, rows), jnp.float32),
            pltpu.VMEM((WIDE, rows), jnp.float32),
        ],
        compiler_params=pltpu.CompilerParams(vmem_limit_bytes=vmem_bytes),
        cost_estimate=pl.CostEstimate(
            flops=4 * rows * length * queries.shape[1], bytes_accessed=8 * length * D,
            transcendentals=rows * length * HEADS // 2,
        ),
    )(seen, queries, kv, kv, *marks)


def pull_attend(seen, queries, kv, d_att, att, log_total, marks):
    rows, length = queries.shape[0], kv.shape[0]
    sub = rows // 2
    pairs = queries.shape[1] // WIDE
    return pl.pallas_call(
        pull_kernel,
        grid=(pairs,),
        in_specs=[
            pl.BlockSpec(memory_space=pltpu.SMEM),
            per_pair(rows), per_pair(length), per_pair(length, PAIRS), per_pair(rows), per_pair(rows),
            pl.BlockSpec((1, 2, rows), lambda pair: (pair, 0, 0)),
            whole((1, rows)), whole((1, rows)), whole((length, 1)), whole((length, 1)),
        ],
        out_specs=[per_pair(rows), pl.BlockSpec((2, length, WIDE), lambda pair: (0, 0, pair))],
        out_shape=[
            jax.ShapeDtypeStruct((rows, queries.shape[1]), jnp.float32),
            jax.ShapeDtypeStruct((2, length, queries.shape[1]), jnp.bfloat16),
        ],
        scratch_shapes=[
            pltpu.VMEM((length, rows), jnp.float32),
            pltpu.VMEM((2, rows, WIDE), jnp.bfloat16),
            pltpu.VMEM((2, rows, WIDE), jnp.bfloat16),
            pltpu.VMEM((2, rows), jnp.float32),
            pltpu.VMEM((2, rows, WIDE), jnp.float32),
            pltpu.VMEM((sub, WIDE), jnp.float32),
            pltpu.VMEM((sub, WIDE), jnp.float32),
        ],
        compiler_params=pltpu.CompilerParams(vmem_limit_bytes=vmem_bytes),
        cost_estimate=pl.CostEstimate(
            flops=10 * rows * length * queries.shape[1], bytes_accessed=12 * length * D,
            transcendentals=rows * length * HEADS // 2,
        ),
    )(seen, queries, kv, kv, d_att, att, log_total, *marks)


def layer_norm(inputs, scale_gain):
    centre = jnp.mean(inputs, -1, keepdims=True)
    shifted = inputs - centre
    spread = jnp.mean(shifted * shifted, -1, keepdims=True)
    return shifted * lax.rsqrt(spread + norm_eps) * scale_gain


def rotary_tables(positions):
    exponents = jnp.arange(HEAD_DIM // 2, dtype=jnp.float32) * (2.0 / HEAD_DIM)
    frequency = jnp.power(jnp.float32(rope_base), -exponents)
    angles = positions.astype(jnp.float32)[:, None] * frequency[None, :]
    cosine, sine = jnp.cos(angles), jnp.sin(angles)
    return (
        jnp.tile(jnp.concatenate([cosine, cosine], 1), (1, HEADS)),
        jnp.tile(jnp.concatenate([-sine, sine], 1), (1, HEADS)),
    )


def rotary(inputs, cosine, signed_sine):
    half = HEAD_DIM // 2
    lane = lax.broadcasted_iota(jnp.int32, inputs.shape, 1) % HEAD_DIM
    swapped = jnp.where(lane < half, jnp.roll(inputs, -half, 1), jnp.roll(inputs, half, 1))
    return inputs * cosine + swapped * signed_sine


def gated_gelu(gate_part, up_part):
    return jax.nn.gelu(gate_part, approximate=False) * up_part


def bits_down(axis):
    count = (lax.axis_size(axis) - 1).bit_length()
    return [(axis, 1 << i) for i in reversed(range(count))]


def swap(array, axis, bit):
    count = lax.axis_size(axis)
    return lax.ppermute(array, axis, [(i, i ^ bit) for i in range(count)])


def bit_here(step):
    return (lax.axis_index(step[0]) // step[1]) % 2


def halve(array, place, step):
    here = bit_here(step)
    kept = lax.dynamic_index_in_dim(array, here, place, True)
    got = swap(lax.dynamic_index_in_dim(array, 1 - here, place, True), *step)
    return (kept.astype(jnp.float32) + got.astype(jnp.float32)).astype(jnp.bfloat16)


def double(array, place, step):
    got = swap(array, *step)
    return jnp.where(
        bit_here(step) == 0,
        jnp.concatenate([array, got], place),
        jnp.concatenate([got, array], place),
    )


def gather(array, places, order):
    array = array.reshape((1,) * len(places) + array.shape)
    for step in order:
        array = double(array, places.index(step), step)
    return array


def gather_rows(array, order):
    ctx_used = [step for step in bits_down("ctx") if step in order]
    share = 0
    for step in ctx_used:
        share = share * 2 + bit_here(step)
    rows = array.shape[0] // 2 ** len(ctx_used)
    part = lax.dynamic_slice_in_dim(array, share * rows, rows)
    return gather(part, bits_down("dp") + ctx_used, order).reshape(-1, array.shape[1])


def owned_sums(parts, order):
    ctx = lax.axis_size("ctx")
    counts = [part.shape[1] for part in parts]
    missing = -sum(counts) % (8 * ctx)
    if missing:
        last = jnp.pad(parts[-1], ((0, 0), (0, missing), (0, 0)))
        parts = parts[:-1] + [last]
    packed = jnp.concatenate(parts, 1) if len(parts) > 1 else parts[0]
    total = packed.shape[1]
    places = bits_down("dp") + bits_down("ctx")
    packed = packed.reshape((2,) * len(places) + (total // ctx, D))
    for step in order:
        packed = halve(packed, places.index(step), step)
    for step in bits_down("ctx"):
        packed = double(packed, places.index(step), step)
    full = packed.reshape(total, D).astype(jnp.float32)
    found, start = [], 0
    for count in counts:
        found.append(full[start : start + count])
        start += count
    return found


def by_owner(array):
    dp = lax.axis_size("dp")
    return array.astype(jnp.bfloat16).reshape(dp, array.shape[0] // dp, D)


def gain_row(array):
    dp = lax.axis_size("dp")
    rows = array.astype(jnp.bfloat16).reshape(dp, 1, D // dp)
    return jnp.pad(rows, ((0, 0), (0, 0), (0, D - D // dp)))


def on_device(
    tokens, doc_ids, pair_table, gain_attn, gain_ffn, w_qkv, w_out, w_in, w_down, cotangent
):
    dp_size, ctx_size = lax.axis_size("dp"), lax.axis_size("ctx")
    ctx_here = lax.axis_index("ctx")
    rows_dev = tokens.shape[1]
    sub = rows_dev // 2
    seq_len = rows_dev * ctx_size
    blocks = 2 * ctx_size
    pair = pair_table.astype(jnp.int32)
    block_ids = jnp.stack([pair, blocks - 1 - pair], 1).reshape(blocks)
    positions = (
        block_ids[:, None] * sub + jnp.arange(sub, dtype=jnp.int32)[None, :]
    ).reshape(seq_len)
    doc_slots = jnp.take(doc_ids[0].reshape(blocks, sub), block_ids, axis=0).reshape(seq_len)
    pos_own = lax.dynamic_slice_in_dim(positions, ctx_here * rows_dev, rows_dev)
    doc_own = lax.dynamic_slice_in_dim(doc_slots, ctx_here * rows_dev, rows_dev)
    ids_own = lax.dynamic_slice_in_dim(block_ids, ctx_here * 2, 2)
    low_doc = doc_slots.reshape(blocks, sub)[:, 0]
    high_doc = doc_slots.reshape(blocks, sub)[:, -1]
    low_own = doc_own.reshape(2, sub)[:, 0]
    seen = (
        ((block_ids[None, :] <= ids_own[:, None]) & (high_doc[None, :] >= low_own[:, None]))
        .astype(jnp.int32)
        .reshape(2 * blocks)
    )
    marks = (
        pos_own.reshape(1, rows_dev), doc_own.reshape(1, rows_dev),
        positions.reshape(seq_len, 1), doc_slots.reshape(seq_len, 1),
    )
    cosine, sine = rotary_tables(pos_own)

    dp_bits, ctx_bits = bits_down("dp"), bits_down("ctx")
    core, far = ctx_bits[-1:], ctx_bits[:-1]
    near_x, along_z = dp_bits[-1:], dp_bits[:-1]
    kv_full = gather_rows(w_qkv[:, D:], dp_bits + ctx_bits)
    share = D // dp_size // ctx_size
    gains_here = jnp.pad(
        jnp.stack([gain_attn, gain_ffn]), ((0, 6), (0, D - D // dp_size))
    )
    q_part = jnp.concatenate(
        [lax.dynamic_slice_in_dim(w_qkv[:, :D], ctx_here * share, share), gains_here], 0
    )
    q_packed = gather(q_part, dp_bits + ctx_bits, along_z + far + near_x + core)
    q_packed = q_packed.reshape(dp_size, ctx_size, share + 8, D)
    q_full = q_packed[:, :, :share].reshape(D, D)
    gains = q_packed[:, 0, share : share + 2, : D // dp_size].astype(jnp.float32)
    gains = gains.transpose(1, 0, 2).reshape(2, D)
    in_full = gather_rows(w_in, dp_bits + core)
    out_rows_here = w_out.shape[0]
    tail = gather_rows(jnp.concatenate([w_out, w_down], 0), dp_bits + core)
    tail = tail.reshape(dp_size, -1, D)
    out_full = tail[:, :out_rows_here].reshape(D, D)
    down_full = tail[:, out_rows_here:].reshape(FF, D)
    x_rows = tokens[0].astype(jnp.float32)
    normed_attn, pull_attn = jax.vjp(layer_norm, x_rows, gains[0])
    normed_low = normed_attn.astype(jnp.bfloat16)
    kv_rows = jnp.dot(normed_low, kv_full, preferred_element_type=jnp.float32)
    keys_own = rotary(kv_rows[:, :D], cosine, sine).astype(jnp.bfloat16)
    kv_own = jnp.concatenate([keys_own, kv_rows[:, D:].astype(jnp.bfloat16)], 1)
    kv_all = gather(kv_own, ctx_bits, ctx_bits).reshape(seq_len, 2 * D)
    q_rows = jnp.dot(normed_low, q_full, preferred_element_type=jnp.float32)
    queries = (rotary(q_rows, cosine, sine) * score_scale).astype(jnp.bfloat16)
    attended_sum, log_total = attend(seen, queries, kv_all, marks)
    attended = attended_sum.astype(jnp.bfloat16)
    mid_rows = x_rows + jnp.dot(attended, out_full, preferred_element_type=jnp.float32)
    normed_ffn, pull_ffn = jax.vjp(layer_norm, mid_rows, gains[1])
    normed_second = normed_ffn.astype(jnp.bfloat16)
    gate_up = jnp.dot(normed_second, in_full, preferred_element_type=jnp.float32)
    mixed_float, pull_mix = jax.vjp(gated_gelu, gate_up[:, :FF], gate_up[:, FF:])
    mixed_low = mixed_float.astype(jnp.bfloat16)
    d_out_low = cotangent[0]
    d_mixed = contract(d_out_low, down_full, 1, 1)
    d_gate, d_up = pull_mix(d_mixed)
    d_gate_up = jnp.concatenate([d_gate, d_up], 1).astype(jnp.bfloat16)
    d_normed_second = contract(d_gate_up, in_full, 1, 1)
    d_mid_norm, grad_ffn_gain = pull_ffn(d_normed_second)
    d_mid = d_out_low.astype(jnp.float32) + d_mid_norm
    d_branch = d_mid.astype(jnp.bfloat16)
    grad_down = contract(mixed_low, d_out_low, 0, 0)
    grad_in = [contract(normed_second, d_gate_up[:, i * D : (i + 1) * D], 0, 0) for i in range(3)]
    grad_out = contract(attended, d_branch, 0, 0)
    in_sums = owned_sums(
        [by_owner(part) for part in grad_in], core + near_x + along_z[::-1] + far
    )
    tail_sums = owned_sums(
        [by_owner(grad_down), by_owner(grad_out), gain_row(grad_ffn_gain)],
        core + far + near_x + along_z[::-1],
    )
    d_att = contract(d_branch, out_full, 1, 1).astype(jnp.bfloat16)
    d_queries, d_kv_all = pull_attend(seen, queries, kv_all, d_att, attended_sum, log_total, marks)
    out_rows = mid_rows + jnp.dot(mixed_low, down_full, preferred_element_type=jnp.float32)
    d_kv = d_kv_all.reshape((2,) + (2,) * len(ctx_bits) + (rows_dev, D))
    for step in core + far:
        d_kv = halve(d_kv, 1 + ctx_bits.index(step), step)
    d_kv = d_kv.reshape(2, rows_dev, D)
    d_q = rotary(d_queries, cosine, -sine).astype(jnp.bfloat16)
    q_sums = owned_sums(
        [by_owner(contract(normed_low, d_q, 0, 0))], core + near_x + far + along_z[::-1]
    )
    d_v = d_kv[1]
    v_sums = owned_sums(
        [by_owner(contract(normed_low, d_v, 0, 0))], core + near_x + far + along_z[::-1]
    )
    d_k = rotary(d_kv[0].astype(jnp.float32), cosine, -sine).astype(jnp.bfloat16)
    d_normed_attn = contract(d_q, q_full, 1, 1) + contract(
        jnp.concatenate([d_k, d_v], 1), kv_full, 1, 1
    )
    d_x_norm, grad_attn_gain = pull_attn(d_normed_attn)
    grad_rows = (d_mid + d_x_norm).astype(jnp.bfloat16)
    k_sums = owned_sums(
        [by_owner(contract(normed_low, d_k, 0, 0)), gain_row(grad_attn_gain)],
        core + far + near_x + along_z[::-1],
    )
    return (
        out_rows.astype(jnp.bfloat16)[None],
        grad_rows[None],
        k_sums[1][0, : D // dp_size],
        tail_sums[2][0, : D // dp_size],
        jnp.concatenate([q_sums[0], k_sums[0], v_sums[0]], 1),
        tail_sums[1],
        jnp.concatenate(in_sums, 1),
        tail_sums[0],
    )


def solution(mesh):
    return jax.shard_map(
        on_device,
        mesh=mesh,
        in_specs=(
            P("dp", "ctx", None),
            P("dp", None),
            P(),
            P("dp"),
            P("dp"),
            P("dp", None),
            P("dp", None),
            P("dp", None),
            P("dp", None),
            P("dp", "ctx", None),
        ),
        out_specs=(
            P("dp", "ctx", None),
            P("dp", "ctx", None),
            P("dp"),
            P("dp"),
            P("dp", None),
            P("dp", None),
            P("dp", None),
            P("dp", None),
        ),
        check_vma=False,
    )
```

time: 911 us -> 464 us (0.51)
  waiting for transfers between devices: 516 us -> 161 us
  matrix products: 183 us -> 37.7 us
  starting transfers between devices: 1.02 us -> 102 us
  blocking collectives: 48.8 us -> 0 us
  local copies, waits for them, and re-layouts: 89.7 us -> 47.4 us
  Pallas kernels: 0 us -> 35.5 us
  other arithmetic: 41.1 us -> 71.4 us
  between operations: 16.3 us -> 2.42 us
    reduce_scatter x6 -> x0, waiting for transfers between devices: 347 us -> none  [the longest x1 82.6 us: on_device(): lax.psum_scatter(grad_qkv.astype(jnp.bfloat16), 'dp', scatter_dimension=0...]
    ppermute x0 -> x57, waiting for transfers between devices: none -> 161 us  [swap(): return lax.ppermute(array, axis, [(i, i ^ bit) for i in range(count)])]
    all_gather x6 -> x0, waiting for transfers between devices: 157 us -> none  [the longest x1 63.3 us: on_device(): lax.all_gather(w_in, 'dp', axis=0, tiled=True)]
    dot_general x37 -> x15, matrix products: 171 us -> 31.4 us  [the longest x13 27.6 us: contract(): lax.dot_general(left, right, (((left_dim,), (right_dim,)), ((), ())), pre...]
    ppermute x0 -> x57, starting transfers between devices: none -> 102 us  [swap(): return lax.ppermute(array, axis, [(i, i ^ bit) for i in range(count)])]
    unnamed x2 -> x0, blocking collectives: 43.2 us -> none
    pallas_call x0 -> x2, Pallas kernels: none -> 35.5 us  [the longest x1 19 us: pull_attend(): pl.pallas_call(pull_kernel, grid=(pairs,), in_specs=[pl.BlockSpec(memory_...]
    select_n x2 -> x32, other arithmetic: 2.62 us -> 33.5 us  [the longest x30 33.4 us: double(): jnp.where(bit_here(step) == 0, jnp.concatenate([array, got], place), jnp....]
  transfers between devices with their start and end apart: 13 -> 57, of which waited for: 13 -> 28; matrix products, arithmetic and copies ran while one was open for 14% -> 22% of each run, Pallas kernels for 0% -> 4%
where the time goes in v1:
time: 464 us; the launch traced here: 458 us
  waiting for transfers between devices  161 us (35%)
  starting transfers between devices  102 us (22%)
  other arithmetic  71.4 us (15%)
  local copies, waits for them, and re-layouts  47.4 us (10%)
  matrix products  37.7 us (8%)
  Pallas kernels  35.5 us (8%)
    ppermute x57, waiting for transfers between devices, swap(): return lax.ppermute(array, axis, [(i, i ^ bit) for i in range(count)])  161 us
    ppermute x57, starting transfers between devices, swap(): return lax.ppermute(array, axis, [(i, i ^ bit) for i in range(count)])  102 us
    select_n x30, other arithmetic, double(): jnp.where(bit_here(step) == 0, jnp.concatenate([array, got], place), jnp....  33.4 us
    dot_general x13, matrix products, contract(): lax.dot_general(left, right, (((left_dim,), (right_dim,)), ((), ())), pre...  27.6 us
    pallas_call x1, Pallas kernels, pull_attend(): pl.pallas_call(pull_kernel, grid=(pairs,), in_specs=[pl.BlockSpec(memory_...  19 us
    pallas_call x1, Pallas kernels, attend(): pl.pallas_call(attend_kernel, grid=(pairs,), in_specs=[pl.BlockSpec(memor...  16.6 us
    unnamed x125, local copies, waits for them, and re-layouts  12.9 us
  transfers between devices with their start and end apart: 57, of which 28 were waited for; matrix products, arithmetic and copies ran while one was open for 22% of the time, Pallas kernels for 4%

profile of v1, /device:TPU:0, one launch (start us, length us, event | category | flops | bytes accessed | tf_op | source)
XLA Modules:
  0.0 457.7 jit_solution(2905773796172647038)
XLA Ops:
  2.4 4.1 collective-permute-start
  9.5 2.9 collective-permute-start.12
  17.9 5.5 %collective-permute-done.5 = bf16[1,1,1,1,1,24,1536]{6,5,4,3,2,1,0:T(8,128)(2,1)S(1)} collective-permute-done((bf16[1,1,1,1,1,24,1536]{6,5,4,3,2,1,0:T(8,128)(2,1)S(1)}, bf16[1,1,1,1,1,24,1536]{6,5,4,3,2,1,0:T(8,128)(2,1)S(1)}, u32[]{:S(2)}, u32[]{:S(2)}) %collective-permute-start.5) | collective-permute-done | bytes 73760 | tf_op jit(solution)/shard_map/ppermute | solution.py:263
  25.2 7.8 %collective-permute-done.6 = bf16[2,1,1,1,1,24,1536]{6,5,0,4,3,2,1:T(8,128)(2,1)S(1)} collective-permute-done((bf16[2,1,1,1,1,24,1536]{6,5,0,4,3,2,1:T(8,128)(2,1)S(1)}, bf16[2,1,1,1,1,24,1536]{6,5,0,4,3,2,1:T(8,128)(2,1)S(1)}, u32[]{:S(2)}, u32[]{:S(2)}) %collective-permute-start.6) | collective-permute-done | bytes 147488 | tf_op jit(solution)/shard_map/ppermute | solution.py:263
  35.4 4.4 collective-permute-done.7
  45.7 2.4 tile.22
  52.5 2.4 maximum_select_fusion.11
  58.8 2.4 fusion.108
  61.8 3.1 maximum_select_fusion.4
  68.6 2.7 fusion.31
  80.6 5.8 %collective-permute-done.13 = bf16[2,1,1,1,120,768]{5,4,3,2,1,0:T(8,128)(2,1)S(1)} collective-permute-done((bf16[2,1,1,1,120,768]{5,4,3,2,1,0:T(8,128)(2,1)S(1)}, bf16[2,1,1,1,120,768]{5,4,3,2,1,0:T(8,128)(2,1)S(1)}, u32[]{:S(2)}, u32[]{:S(2)}) %collective-permute-start.13) | collective-permute-done | bytes 368672 | tf_op jit(solution)/shard_map/ppermute | solution.py:263
  88.2 6.4 %collective-permute-done.17 = bf16[2,1,1,1,48,2304]{5,4,3,2,1,0:T(8,128)(2,1)S(1)} collective-permute-done((bf16[2,1,1,1,48,2304]{5,4,3,2,1,0:T(8,128)(2,1)S(1)}, bf16[2,1,1,1,48,2304]{5,4,3,2,1,0:T(8,128)(2,1)S(1)}, u32[]{:S(2)}, u32[]{:S(2)}) %collective-permute-start.17) | collective-permute-done | bytes 442400 | tf_op jit(solution)/shard_map/ppermute | solution.py:263
  96.3 11.6 %collective-permute-done.10 = bf16[1,1,512,1536]{3,2,1,0:T(8,128)(2,1)} collective-permute-done((bf16[1,1,512,1536]{3,2,1,0:T(8,128)(2,1)S(1)}, bf16[1,1,512,1536]{3,2,1,0:T(8,128)(2,1)}, u32[]{:S(2)}, u32[]{:S(2)}) %collective-permute-start.10) | collective-permute-done | bytes 1572896 | tf_op jit(solution)/shard_map/ppermute | solution.py:263
  107.9 2.4 maximum_select_fusion.2
  112.3 9.3 %collective-permute-done.18 = bf16[2,2,1,1,48,2304]{5,4,3,2,1,0:T(8,128)(2,1)S(1)} collective-permute-done((bf16[2,2,1,1,48,2304]{5,4,3,2,1,0:T(8,128)(2,1)S(1)}, bf16[2,2,1,1,48,2304]{5,4,3,2,1,0:T(8,128)(2,1)S(1)}, u32[]{:S(2)}, u32[]{:S(2)}) %collective-permute-start.18) | collective-permute-done | bytes 884768 | tf_op jit(solution)/shard_map/ppermute | solution.py:263
  127.4 3.3 maximum_select_fusion.3
  130.9 5.4 %maximum_select_fusion.1 = bf16[2,2,2,2,48,2304]{5,4,3,2,1,0:T(8,128)(2,1)} fusion(bf16[2,2,2,1,48,2304]{5,4,3,2,1,0:T(8,128)(2,1)} %collective-permute-done.19, bf16[2,2,2,1,48,2304]{5,4,3,2,1,0:T(8,128)(2,1)} %maximum_select_fusion.5, pred[]{:T(512)S(6)} %eq.107), kind=kLoop, calls=%fused_computation.5 | loop fusion | flops 5308416 | bytes 7077889 | tf_op jit(solution)/shard_map/jit(_where)/select_n | solution.py:279
  136.3 6.9 %maximum_select_fusion = bf16[2,2,512,1536]{3,2,1,0:T(8,128)(2,1)} fusion(bf16[2,1,512,1536]{3,2,1,0:T(8,128)(2,1)} %collective-permute-done.11, bf16[2,1,512,1536]{3,2,1,0:T(8,128)(2,1)S(1)} %maximum_select_fusion.2, pred[]{:T(512)S(6)} %eq.107), kind=kLoop, calls=%fused_computation.2 | loop fusion | flops 9437184 | bytes 12582913 | tf_op jit(solution)/shard_map/jit(_where)/select_n | solution.py:279
  143.2 16.6 %shard_map.161 = (f32[512,768]{1,0:T(8,128)}, f32[6,2,512]{2,1,0:T(2,128)}) custom-call(s32[16]{0:T(128)} %reshape.3497.seen_ref, bf16[512,768]{1,0:T(8,128)(2,1)} %get-tuple-element.37.q_ref, bf16[2048,1536]{1,0:T(8,128)(2,1)} %bitcast.226, bf16[2048,1536]{1,0:T(8,128)(2,1)} %bitcast.227, s32[1,512]{1,0:T(1,128)} %bitcast.290, s32[1,512]{1,0:T(1,128)} %bitcast.286, ...), custom_call_target="tpu_custom_call" | custom-call | flops 3221225472 | bytes 12582912 | tf_op jit(solution)/shard_map/pallas_call | solution.py:165
  159.8 2.3 fusion.123
  166.1 6.1 %add_convert_fusion.4 = (bf16[512,1152]{1,0:T(8,128)(2,1)S(1)}, f32[512,1152]{1,0:T(8,128)S(1)}, f32[512,1152]{1,0:T(8,128)S(1)}) fusion(f32[512,2304]{1,0:T(8,128)S(1)} %fusion.124, bf16[1152,768]{1,0:T(8,128)(2,1)S(1)} %bitcast.261, bf16[1,512,768]{2,1,0:T(8,128)(2,1)S(1)} %copy-done.21), kind=kOutput, calls=%fused_computation.30 | convolution fusion | flops 949026816 | bytes 13172736 | tf_op jit(solution)/shard_map/dot_general | solution.py:25
  179.5 2.4 multiply_reduce_fusion
  185.9 2.7 convolution_convert_fusion
  191.3 18.1 %collective-permute-start.29 = (bf16[2,2,2,2,1,64,768]{6,5,4,3,2,1,0:T(8,128)(2,1)}, bf16[2,2,2,2,1,64,768]{6,5,4,3,2,1,0:T(8,128)(2,1)}, u32[]{:S(2)}, u32[]{:S(2)}) collective-permute-start(bf16[2,2,2,2,1,64,768]{6,5,4,3,2,1,0:T(8,128)(2,1)} %constant_dynamic-slice_fusion.19), channel_id=1, source_target_pairs={{0,1},{1,0},{2,3},{3,2},{4,5},{5,4},{6,7},{7,6},{8,9},{9,8},{10,11... | collective-permute-start | bytes 4718600 | tf_op jit(solution)/shard_map/ppermute | solution.py:263
  213.8 19.0 %shard_map.162 = (f32[512,768]{1,0:T(8,128)}, bf16[2,2048,768]{2,1,0:T(8,128)(2,1)}) custom-call(s32[16]{0:T(128)} %reshape.3497.seen_ref, bf16[512,768]{1,0:T(8,128)(2,1)} %get-tuple-element.37.q_ref, bf16[2048,1536]{1,0:T(8,128)(2,1)} %bitcast.228, bf16[2048,1536]{1,0:T(8,128)(2,1)} %bitcast.229, bf16[512,768]{1,0:T(8,128)(2,1)} %convolution_convert_fusion.8.datt_ref, ...), custom_call_target="tpu_custom_call" | custom-call | flops 8053063680 | bytes 18874368 | tf_op jit(solution)/shard_map/pallas_call | solution.py:196
  235.0 22.2 %collective-permute-start.20 = (bf16[2,2,1,512,768]{4,3,2,1,0:T(8,128)(2,1)S(1)}, bf16[2,2,1,512,768]{4,3,2,1,0:T(8,128)(2,1)S(1)}, u32[]{:S(2)}, u32[]{:S(2)}) collective-permute-start(bf16[2,2,1,512,768]{4,3,2,1,0:T(8,128)(2,1)S(1)} %constant_dynamic-slice_fusion.26), channel_id=1, source_target_pairs={{0,1},{1,0},{2,3},{3,2},{4,5},{5,4},{6,7},{7,6},{8,9},{9,8},{10,11... | collective-permute-start | bytes 9437192 | tf_op jit(solution)/shard_map/ppermute | solution.py:263
  263.1 16.1 %collective-permute-done.30 = bf16[2,2,2,1,1,64,768]{6,5,4,3,2,1,0:T(8,128)(2,1)S(1)} collective-permute-done((bf16[2,2,2,1,1,64,768]{6,5,4,3,2,1,0:T(8,128)(2,1)S(1)}, bf16[2,2,2,1,1,64,768]{6,5,4,3,2,1,0:T(8,128)(2,1)S(1)}, u32[]{:S(2)}, u32[]{:S(2)}) %collective-permute-start.30) | collective-permute-done | bytes 786464 | tf_op jit(solution)/shard_map/ppermute | solution.py:263
  281.6 12.0 %collective-permute-done.31 = bf16[2,2,1,1,1,64,768]{6,5,4,3,2,1,0:T(8,128)(2,1)S(1)} collective-permute-done((bf16[2,2,1,1,1,64,768]{6,5,4,3,2,1,0:T(8,128)(2,1)S(1)}, bf16[2,2,1,1,1,64,768]{6,5,4,3,2,1,0:T(8,128)(2,1)S(1)}, u32[]{:S(2)}, u32[]{:S(2)}) %collective-permute-start.31) | collective-permute-done | bytes 393248 | tf_op jit(solution)/shard_map/ppermute | solution.py:263
  296.2 5.4 %collective-permute-done.32 = bf16[2,1,1,1,1,64,768]{6,5,4,3,2,1,0:T(8,128)(2,1)S(1)} collective-permute-done((bf16[2,1,1,1,1,64,768]{6,5,4,3,2,1,0:T(8,128)(2,1)S(1)}, bf16[2,1,1,1,1,64,768]{6,5,4,3,2,1,0:T(8,128)(2,1)S(1)}, u32[]{:S(2)}, u32[]{:S(2)}) %collective-permute-start.32) | collective-permute-done | bytes 196640 | tf_op jit(solution)/shard_map/ppermute | solution.py:263
  301.7 8.1 %collective-permute-start.33 = (bf16[1,1,1,1,1,64,768]{6,5,4,3,2,1,0:T(8,128)(2,1)S(1)}, bf16[1,1,1,1,1,64,768]{6,5,4,3,2,1,0:T(8,128)(2,1)S(1)}, u32[]{:S(2)}, u32[]{:S(2)}) collective-permute-start(bf16[1,1,1,1,1,64,768]{6,5,4,3,2,1,0:T(8,128)(2,1)S(1)} %constant_dynamic-slice_fusion.15), channel_id=1, source_target_pairs={{0,16},{4,20},{8,24},{12,28},{16,0},{20,4},{24,8},{28,12},{1,17},{... | collective-permute-start | bytes 294920 | tf_op jit(solution)/shard_map/ppermute | solution.py:263
  310.0 2.5 collective-permute-done.33
  313.2 6.0 %collective-permute-start.53 = (bf16[1,1,1,2,1,72,768]{6,5,4,3,2,1,0:T(8,128)(2,1)S(1)}, bf16[1,1,1,2,1,72,768]{6,5,4,3,2,1,0:T(8,128)(2,1)S(1)}, u32[]{:S(2)}, u32[]{:S(2)}) collective-permute-start(bf16[1,1,1,2,1,72,768]{6,5,4,3,2,1,0:T(8,128)(2,1)S(1)} %constant_dynamic-slice_fusion.1), channel_id=1, source_target_pairs={{0,16},{4,20},{8,24},{12,28},{16,0},{20,4},{24,8},{28,12},{1,17},{... | collective-permute-start | bytes 663560 | tf_op jit(solution)/shard_map/ppermute | solution.py:263
  320.6 8.4 %collective-permute-done.53 = bf16[1,1,1,2,1,72,768]{6,5,4,3,2,1,0:T(8,128)(2,1)S(1)} collective-permute-done((bf16[1,1,1,2,1,72,768]{6,5,4,3,2,1,0:T(8,128)(2,1)S(1)}, bf16[1,1,1,2,1,72,768]{6,5,4,3,2,1,0:T(8,128)(2,1)S(1)}, u32[]{:S(2)}, u32[]{:S(2)}) %collective-permute-start.53) | collective-permute-done | bytes 221216 | tf_op jit(solution)/shard_map/ppermute | solution.py:263
  329.4 28.3 %collective-permute-done.54 = bf16[1,1,1,1,1,72,768]{6,5,4,3,2,1,0:T(8,128)(2,1)S(1)} collective-permute-done((bf16[1,1,1,1,1,72,768]{6,5,4,3,2,1,0:T(8,128)(2,1)S(1)}, bf16[1,1,1,1,1,72,768]{6,5,4,3,2,1,0:T(8,128)(2,1)S(1)}, u32[]{:S(2)}, u32[]{:S(2)}) %collective-permute-start.54) | collective-permute-done | bytes 110624 | tf_op jit(solution)/shard_map/ppermute | solution.py:263
  359.7 2.9 collective-permute-done.55
  370.4 3.0 add_convert_fusion.10
  376.8 3.1 copy.88
  379.8 3.0 copy.89
  382.9 3.1 copy.87
  385.9 2.8 add_convert_fusion.8
  392.3 2.8 fusion.22
  406.2 5.9 %collective-permute-done.37 = bf16[2,2,1,2,1,24,768]{6,5,4,3,2,1,0:T(8,128)(2,1)S(1)} collective-permute-done((bf16[2,2,1,2,1,24,768]{6,5,4,3,2,1,0:T(8,128)(2,1)S(1)}, bf16[2,2,1,2,1,24,768]{6,5,4,3,2,1,0:T(8,128)(2,1)S(1)}, u32[]{:S(2)}, u32[]{:S(2)}) %collective-permute-start.37) | collective-permute-done | bytes 294944 | tf_op jit(solution)/shard_map/ppermute | solution.py:263
  412.6 5.1 %collective-permute-done.44 = bf16[2,2,1,2,1,24,768]{6,5,4,3,2,1,0:T(8,128)(2,1)S(1)} collective-permute-done((bf16[2,2,1,2,1,24,768]{6,5,4,3,2,1,0:T(8,128)(2,1)S(1)}, bf16[2,2,1,2,1,24,768]{6,5,4,3,2,1,0:T(8,128)(2,1)S(1)}, u32[]{:S(2)}, u32[]{:S(2)}) %collective-permute-start.44) | collective-permute-done | bytes 294944 | tf_op jit(solution)/shard_map/ppermute | solution.py:263
  419.8 3.3 collective-permute-start.39
  423.2 3.2 collective-permute-start.46
  442.0 3.0 collective-permute-done.25
  446.9 3.1 collective-permute-done.26
  450.1 2.4 collective-permute-start.27
  (409 shorter events, 143.9 us)
Async XLA Ops:
  2.4 13.5 %collective-permute-start = (bf16[1,1,1,1,1,32,768]{6,5,4,3,2,1,0:T(8,128)(2,1)S(1)}, bf16[1,1,1,1,1,32,768]{6,5,4,3,2,1,0:T(8,128)(2,1)S(1)}, u32[]{:S(2)}, u32[]{:S(2)}) collective-permute-start(bf16[1,1,1,1,1,32,768]{6,5,4,3,2,1,0:T(8,128)(2,1)S(1)} %get-tuple-element.82), channel_id=1, source_target_pairs={{0,16},{4,20},{8,24},{12,28},{16,0},{20,4},{24,8},{28,12},{1,17},{... | collective-permute-start | bytes 147464 | tf_op jit(solution)/shard_map/ppermute | solution.py:263
  7.5 15.9 %collective-permute-start.5 = (bf16[1,1,1,1,1,24,1536]{6,5,4,3,2,1,0:T(8,128)(2,1)S(1)}, bf16[1,1,1,1,1,24,1536]{6,5,4,3,2,1,0:T(8,128)(2,1)S(1)}, u32[]{:S(2)}, u32[]{:S(2)}) collective-permute-start(bf16[1,1,1,1,1,24,1536]{6,5,4,3,2,1,0:T(8,128)(2,1)S(1)} %get-tuple-element.71), channel_id=1, source_target_pairs={{0,16},{4,20},{8,24},{12,28},{16,0},{20,4},{24,8},{28,12},{1,17},{... | collective-permute-start | bytes 221192 | tf_op jit(solution)/shard_map/ppermute | solution.py:263
  9.5 64.1 %collective-permute-start.12 = (bf16[1,1,1,1,120,768]{5,4,3,2,1,0:T(8,128)(2,1)}, bf16[1,1,1,1,120,768]{5,4,3,2,1,0:T(8,128)(2,1)}, u32[]{:S(2)}, u32[]{:S(2)}) collective-permute-start(bf16[1,1,1,1,120,768]{5,4,3,2,1,0:T(8,128)(2,1)} %get-tuple-element.67), channel_id=1, source_target_pairs={{0,16},{4,20},{8,24},{12,28},{16,0},{20,4},{24,8},{28,12},{1,17},{... | collective-permute-start | bytes 552968 | tf_op jit(solution)/shard_map/ppermute | solution.py:263
  13.2 62.9 %collective-permute-start.16 = (bf16[1,1,1,1,48,2304]{5,4,3,2,1,0:T(8,128)(2,1)}, bf16[1,1,1,1,48,2304]{5,4,3,2,1,0:T(8,128)(2,1)}, u32[]{:S(2)}, u32[]{:S(2)}) collective-permute-start(bf16[1,1,1,1,48,2304]{5,4,3,2,1,0:T(8,128)(2,1)} %get-tuple-element.63), channel_id=1, source_target_pairs={{0,16},{4,20},{8,24},{12,28},{16,0},{20,4},{24,8},{28,12},{1,17},{... | collective-permute-start | bytes 663560 | tf_op jit(solution)/shard_map/ppermute | solution.py:263
  16.0 7.6 %collective-permute-start.1 = (bf16[2,1,1,1,1,32,768]{6,5,4,3,2,1,0:T(8,128)(2,1)S(1)}, bf16[2,1,1,1,1,32,768]{6,5,4,3,2,1,0:T(8,128)(2,1)S(1)}, u32[]{:S(2)}, u32[]{:S(2)}) collective-permute-start(bf16[2,1,1,1,1,32,768]{6,5,4,3,2,1,0:T(8,128)(2,1)S(1)} %maximum_select_fusion.39), channel_id=1, source_target_pairs={{0,8},{4,12},{8,0},{12,4},{16,24},{20,28},{24,16},{28,20},{1,9},{5... | collective-permute-start | bytes 294920 | tf_op jit(solution)/shard_map/ppermute | solution.py:263
  23.4 9.6 %collective-permute-start.6 = (bf16[2,1,1,1,1,24,1536]{6,5,0,4,3,2,1:T(8,128)(2,1)S(1)}, bf16[2,1,1,1,1,24,1536]{6,5,0,4,3,2,1:T(8,128)(2,1)S(1)}, u32[]{:S(2)}, u32[]{:S(2)}) collective-permute-start(bf16[2,1,1,1,1,24,1536]{6,5,0,4,3,2,1:T(8,128)(2,1)S(1)} %fusion.64), channel_id=1, source_target_pairs={{0,8},{4,12},{8,0},{12,4},{16,24},{20,28},{24,16},{28,20},{1,9},{5... | collective-permute-start | bytes 442376 | tf_op jit(solution)/shard_map/ppermute | solution.py:263
  23.6 11.0 %collective-permute-start.2 = (bf16[2,2,1,1,1,32,768]{6,5,4,3,2,1,0:T(8,128)(2,1)S(1)}, bf16[2,2,1,1,1,32,768]{6,5,4,3,2,1,0:T(8,128)(2,1)S(1)}, u32[]{:S(2)}, u32[]{:S(2)}) collective-permute-start(bf16[2,2,1,1,1,32,768]{6,5,4,3,2,1,0:T(8,128)(2,1)S(1)} %maximum_select_fusion.31), channel_id=1, source_target_pairs={{0,2},{1,3},{2,0},{3,1},{4,6},{5,7},{6,4},{7,5},{8,10},{9,11},{10,... | collective-permute-start | bytes 589832 | tf_op jit(solution)/shard_map/ppermute | solution.py:263
  33.1 6.8 %collective-permute-start.7 = (bf16[2,2,1,1,1,24,1536]{6,5,4,3,2,1,0:T(8,128)(2,1)S(1)}, bf16[2,2,1,1,1,24,1536]{6,5,4,3,2,1,0:T(8,128)(2,1)S(1)}, u32[]{:S(2)}, u32[]{:S(2)}) collective-permute-start(bf16[2,2,1,1,1,24,1536]{6,5,4,3,2,1,0:T(8,128)(2,1)S(1)} %copy.73), channel_id=1, source_target_pairs={{0,4},{4,0},{8,12},{12,8},{16,20},{20,16},{24,28},{28,24},{1,5},{5... | collective-permute-start | bytes 884744 | tf_op jit(solution)/shard_map/ppermute | solution.py:263
  34.7 9.3 %collective-permute-start.3 = (bf16[2,2,1,2,1,32,768]{6,5,4,3,2,1,0:T(8,128)(2,1)S(1)}, bf16[2,2,1,2,1,32,768]{6,5,4,3,2,1,0:T(8,128)(2,1)S(1)}, u32[]{:S(2)}, u32[]{:S(2)}) collective-permute-start(bf16[2,2,1,2,1,32,768]{6,5,4,3,2,1,0:T(8,128)(2,1)S(1)} %maximum_select_fusion.23), channel_id=1, source_target_pairs={{0,4},{4,0},{8,12},{12,8},{16,20},{20,16},{24,28},{28,24},{1,5},{5... | collective-permute-start | bytes 1179656 | tf_op jit(solution)/shard_map/ppermute | solution.py:263
  40.8 11.7 %collective-permute-start.8 = (bf16[2,2,2,1,1,24,1536]{6,5,4,3,2,1,0:T(8,128)(2,1)}, bf16[2,2,2,1,1,24,1536]{6,5,4,3,2,1,0:T(8,128)(2,1)}, u32[]{:S(2)}, u32[]{:S(2)}) collective-permute-start(bf16[2,2,2,1,1,24,1536]{6,5,4,3,2,1,0:T(8,128)(2,1)} %maximum_select_fusion.18), channel_id=1, source_target_pairs={{0,2},{1,3},{2,0},{3,1},{4,6},{5,7},{6,4},{7,5},{8,10},{9,11},{10,... | collective-permute-start | bytes 1769480 | tf_op jit(solution)/shard_map/ppermute | solution.py:263
  45.0 10.4 %collective-permute-start.4 = (bf16[2,2,2,2,1,32,768]{6,5,4,3,2,1,0:T(8,128)(2,1)}, bf16[2,2,2,2,1,32,768]{6,5,4,3,2,1,0:T(8,128)(2,1)}, u32[]{:S(2)}, u32[]{:S(2)}) collective-permute-start(bf16[2,2,2,2,1,32,768]{6,5,4,3,2,1,0:T(8,128)(2,1)} %maximum_select_fusion.14), channel_id=1, source_target_pairs={{0,1},{1,0},{2,3},{3,2},{4,5},{5,4},{6,7},{7,6},{8,9},{9,8},{10,11... | collective-permute-start | bytes 2359304 | tf_op jit(solution)/shard_map/ppermute | solution.py:263
  54.9 6.9 %collective-permute-start.9 = (bf16[2,2,2,2,1,24,1536]{6,5,4,3,2,1,0:T(8,128)(2,1)}, bf16[2,2,2,2,1,24,1536]{6,5,4,3,2,1,0:T(8,128)(2,1)}, u32[]{:S(2)}, u32[]{:S(2)}) collective-permute-start(bf16[2,2,2,2,1,24,1536]{6,5,4,3,2,1,0:T(8,128)(2,1)} %maximum_select_fusion.11), channel_id=1, source_target_pairs={{0,1},{1,0},{2,3},{3,2},{4,5},{5,4},{6,7},{7,6},{8,9},{9,8},{10,11... | collective-permute-start | bytes 3538952 | tf_op jit(solution)/shard_map/ppermute | solution.py:263
  71.5 36.5 %collective-permute-start.10 = (bf16[1,1,512,1536]{3,2,1,0:T(8,128)(2,1)S(1)}, bf16[1,1,512,1536]{3,2,1,0:T(8,128)(2,1)}, u32[]{:S(2)}, u32[]{:S(2)}) collective-permute-start(bf16[1,1,512,1536]{3,2,1,0:T(8,128)(2,1)S(1)} %maximum_bitcast_fusion), channel_id=1, source_target_pairs={{0,2},{1,3},{2,0},{3,1},{4,6},{5,7},{6,4},{7,5},{8,10},{9,11},{10,... | collective-permute-start | bytes 4718600 | tf_op jit(solution)/shard_map/ppermute | solution.py:263
  74.9 11.6 %collective-permute-start.13 = (bf16[2,1,1,1,120,768]{5,4,3,2,1,0:T(8,128)(2,1)S(1)}, bf16[2,1,1,1,120,768]{5,4,3,2,1,0:T(8,128)(2,1)S(1)}, u32[]{:S(2)}, u32[]{:S(2)}) collective-permute-start(bf16[2,1,1,1,120,768]{5,4,3,2,1,0:T(8,128)(2,1)S(1)} %maximum_select_fusion.26), channel_id=1, source_target_pairs={{0,8},{4,12},{8,0},{12,4},{16,24},{20,28},{24,16},{28,20},{1,9},{5... | collective-permute-start | bytes 1105928 | tf_op jit(solution)/shard_map/ppermute | solution.py:263
  77.4 17.2 %collective-permute-start.17 = (bf16[2,1,1,1,48,2304]{5,4,3,2,1,0:T(8,128)(2,1)S(1)}, bf16[2,1,1,1,48,2304]{5,4,3,2,1,0:T(8,128)(2,1)S(1)}, u32[]{:S(2)}, u32[]{:S(2)}) collective-permute-start(bf16[2,1,1,1,48,2304]{5,4,3,2,1,0:T(8,128)(2,1)S(1)} %maximum_select_fusion.20), channel_id=1, source_target_pairs={{0,8},{4,12},{8,0},{12,4},{16,24},{20,28},{24,16},{28,20},{1,9},{5... | collective-permute-start | bytes 1327112 | tf_op jit(solution)/shard_map/ppermute | solution.py:263
  86.5 24.0 %collective-permute-start.14 = (bf16[2,2,1,1,120,768]{5,4,3,2,1,0:T(8,128)(2,1)S(1)}, bf16[2,2,1,1,120,768]{5,4,3,2,1,0:T(8,128)(2,1)S(1)}, u32[]{:S(2)}, u32[]{:S(2)}) collective-permute-start(bf16[2,2,1,1,120,768]{5,4,3,2,1,0:T(8,128)(2,1)S(1)} %maximum_select_fusion.16), channel_id=1, source_target_pairs={{0,4},{4,0},{8,12},{12,8},{16,20},{20,16},{24,28},{28,24},{1,5},{5... | collective-permute-start | bytes 2211848 | tf_op jit(solution)/shard_map/ppermute | solution.py:263
  94.8 26.9 %collective-permute-start.18 = (bf16[2,2,1,1,48,2304]{5,4,3,2,1,0:T(8,128)(2,1)S(1)}, bf16[2,2,1,1,48,2304]{5,4,3,2,1,0:T(8,128)(2,1)S(1)}, u32[]{:S(2)}, u32[]{:S(2)}) collective-permute-start(bf16[2,2,1,1,48,2304]{5,4,3,2,1,0:T(8,128)(2,1)S(1)} %maximum_select_fusion.13), channel_id=1, source_target_pairs={{0,4},{4,0},{8,12},{12,8},{16,20},{20,16},{24,28},{28,24},{1,5},{5... | collective-permute-start | bytes 2654216 | tf_op jit(solution)/shard_map/ppermute | solution.py:263
  110.3 26.0 %collective-permute-start.11 = (bf16[2,1,512,1536]{3,2,1,0:T(8,128)(2,1)S(1)}, bf16[2,1,512,1536]{3,2,1,0:T(8,128)(2,1)}, u32[]{:S(2)}, u32[]{:S(2)}) collective-permute-start(bf16[2,1,512,1536]{3,2,1,0:T(8,128)(2,1)S(1)} %maximum_select_fusion.2), channel_id=1, source_target_pairs={{0,1},{1,0},{2,3},{3,2},{4,5},{5,4},{6,7},{7,6},{8,9},{9,8},{10,11... | collective-permute-start | bytes 9437192 | tf_op jit(solution)/shard_map/ppermute | solution.py:263
  111.8 15.5 %collective-permute-start.15 = (bf16[2,2,2,1,120,768]{5,4,3,2,1,0:T(8,128)(2,1)}, bf16[2,2,2,1,120,768]{5,4,3,2,1,0:T(8,128)(2,1)}, u32[]{:S(2)}, u32[]{:S(2)}) collective-permute-start(bf16[2,2,2,1,120,768]{5,4,3,2,1,0:T(8,128)(2,1)} %maximum_select_fusion.10), channel_id=1, source_target_pairs={{0,1},{1,0},{2,3},{3,2},{4,5},{5,4},{6,7},{7,6},{8,9},{9,8},{10,11... | collective-permute-start | bytes 4423688 | tf_op jit(solution)/shard_map/ppermute | solution.py:263
  123.1 7.8 %collective-permute-start.19 = (bf16[2,2,2,1,48,2304]{5,4,3,2,1,0:T(8,128)(2,1)}, bf16[2,2,2,1,48,2304]{5,4,3,2,1,0:T(8,128)(2,1)}, u32[]{:S(2)}, u32[]{:S(2)}) collective-permute-start(bf16[2,2,2,1,48,2304]{5,4,3,2,1,0:T(8,128)(2,1)} %maximum_select_fusion.5), channel_id=1, source_target_pairs={{0,1},{1,0},{2,3},{3,2},{4,5},{5,4},{6,7},{7,6},{8,9},{9,8},{10,11... | collective-permute-start | bytes 5308424 | tf_op jit(solution)/shard_map/ppermute | solution.py:263
  191.3 65.9 %collective-permute-start.29 = (bf16[2,2,2,2,1,64,768]{6,5,4,3,2,1,0:T(8,128)(2,1)}, bf16[2,2,2,2,1,64,768]{6,5,4,3,2,1,0:T(8,128)(2,1)}, u32[]{:S(2)}, u32[]{:S(2)}) collective-permute-start(bf16[2,2,2,2,1,64,768]{6,5,4,3,2,1,0:T(8,128)(2,1)} %constant_dynamic-slice_fusion.19), channel_id=1, source_target_pairs={{0,1},{1,0},{2,3},{3,2},{4,5},{5,4},{6,7},{7,6},{8,9},{9,8},{10,11... | collective-permute-start | bytes 4718600 | tf_op jit(solution)/shard_map/ppermute | solution.py:263
  211.0 49.9 %collective-permute-start.50 = (bf16[2,2,2,2,1,72,768]{6,5,4,3,2,1,0:T(8,128)(2,1)}, bf16[2,2,2,2,1,72,768]{6,5,4,3,2,1,0:T(8,128)(2,1)}, u32[]{:S(2)}, u32[]{:S(2)}) collective-permute-start(bf16[2,2,2,2,1,72,768]{6,5,4,3,2,1,0:T(8,128)(2,1)} %constant_dynamic-slice_fusion.4), channel_id=1, source_target_pairs={{0,1},{1,0},{2,3},{3,2},{4,5},{5,4},{6,7},{7,6},{8,9},{9,8},{10,11... | collective-permute-start | bytes 5308424 | tf_op jit(solution)/shard_map/ppermute | solution.py:263
  235.0 84.3 %collective-permute-start.20 = (bf16[2,2,1,512,768]{4,3,2,1,0:T(8,128)(2,1)S(1)}, bf16[2,2,1,512,768]{4,3,2,1,0:T(8,128)(2,1)S(1)}, u32[]{:S(2)}, u32[]{:S(2)}) collective-permute-start(bf16[2,2,1,512,768]{4,3,2,1,0:T(8,128)(2,1)S(1)} %constant_dynamic-slice_fusion.26), channel_id=1, source_target_pairs={{0,1},{1,0},{2,3},{3,2},{4,5},{5,4},{6,7},{7,6},{8,9},{9,8},{10,11... | collective-permute-start | bytes 9437192 | tf_op jit(solution)/shard_map/ppermute | solution.py:263
  259.1 20.0 %collective-permute-start.30 = (bf16[2,2,2,1,1,64,768]{6,5,4,3,2,1,0:T(8,128)(2,1)S(1)}, bf16[2,2,2,1,1,64,768]{6,5,4,3,2,1,0:T(8,128)(2,1)S(1)}, u32[]{:S(2)}, u32[]{:S(2)}) collective-permute-start(bf16[2,2,2,1,1,64,768]{6,5,4,3,2,1,0:T(8,128)(2,1)S(1)} %constant_dynamic-slice_fusion.18), channel_id=1, source_target_pairs={{0,2},{1,3},{2,0},{3,1},{4,6},{5,7},{6,4},{7,5},{8,10},{9,11},{10,... | collective-permute-start | bytes 2359304 | tf_op jit(solution)/shard_map/ppermute | solution.py:263
  263.0 31.4 %collective-permute-start.51 = (bf16[2,2,1,2,1,72,768]{6,5,4,3,2,1,0:T(8,128)(2,1)S(1)}, bf16[2,2,1,2,1,72,768]{6,5,4,3,2,1,0:T(8,128)(2,1)S(1)}, u32[]{:S(2)}, u32[]{:S(2)}) collective-permute-start(bf16[2,2,1,2,1,72,768]{6,5,4,3,2,1,0:T(8,128)(2,1)S(1)} %constant_dynamic-slice_fusion.3), channel_id=1, source_target_pairs={{0,4},{4,0},{8,12},{12,8},{16,20},{20,16},{24,28},{28,24},{1,5},{5... | collective-permute-start | bytes 2654216 | tf_op jit(solution)/shard_map/ppermute | solution.py:263
  279.4 14.2 %collective-permute-start.31 = (bf16[2,2,1,1,1,64,768]{6,5,4,3,2,1,0:T(8,128)(2,1)S(1)}, bf16[2,2,1,1,1,64,768]{6,5,4,3,2,1,0:T(8,128)(2,1)S(1)}, u32[]{:S(2)}, u32[]{:S(2)}) collective-permute-start(bf16[2,2,1,1,1,64,768]{6,5,4,3,2,1,0:T(8,128)(2,1)S(1)} %constant_dynamic-slice_fusion.17), channel_id=1, source_target_pairs={{0,4},{4,0},{8,12},{12,8},{16,20},{20,16},{24,28},{28,24},{1,5},{5... | collective-permute-start | bytes 1179656 | tf_op jit(solution)/shard_map/ppermute | solution.py:263
  293.7 7.9 %collective-permute-start.32 = (bf16[2,1,1,1,1,64,768]{6,5,4,3,2,1,0:T(8,128)(2,1)S(1)}, bf16[2,1,1,1,1,64,768]{6,5,4,3,2,1,0:T(8,128)(2,1)S(1)}, u32[]{:S(2)}, u32[]{:S(2)}) collective-permute-start(bf16[2,1,1,1,1,64,768]{6,5,4,3,2,1,0:T(8,128)(2,1)S(1)} %constant_dynamic-slice_fusion.16), channel_id=1, source_target_pairs={{0,8},{4,12},{8,0},{12,4},{16,24},{20,28},{24,16},{28,20},{1,9},{5... | collective-permute-start | bytes 589832 | tf_op jit(solution)/shard_map/ppermute | solution.py:263
  294.7 18.4 %collective-permute-start.52 = (bf16[2,1,1,2,1,72,768]{6,5,4,3,2,1,0:T(8,128)(2,1)S(1)}, bf16[2,1,1,2,1,72,768]{6,5,4,3,2,1,0:T(8,128)(2,1)S(1)}, u32[]{:S(2)}, u32[]{:S(2)}) collective-permute-start(bf16[2,1,1,2,1,72,768]{6,5,4,3,2,1,0:T(8,128)(2,1)S(1)} %constant_dynamic-slice_fusion.2), channel_id=1, source_target_pairs={{0,8},{4,12},{8,0},{12,4},{16,24},{20,28},{24,16},{28,20},{1,9},{5... | collective-permute-start | bytes 1327112 | tf_op jit(solution)/shard_map/ppermute | solution.py:263
  301.7 10.7 %collective-permute-start.33 = (bf16[1,1,1,1,1,64,768]{6,5,4,3,2,1,0:T(8,128)(2,1)S(1)}, bf16[1,1,1,1,1,64,768]{6,5,4,3,2,1,0:T(8,128)(2,1)S(1)}, u32[]{:S(2)}, u32[]{:S(2)}) collective-permute-start(bf16[1,1,1,1,1,64,768]{6,5,4,3,2,1,0:T(8,128)(2,1)S(1)} %constant_dynamic-slice_fusion.15), channel_id=1, source_target_pairs={{0,16},{4,20},{8,24},{12,28},{16,0},{20,4},{24,8},{28,12},{1,17},{... | collective-permute-start | bytes 294920 | tf_op jit(solution)/shard_map/ppermute | solution.py:263
  312.5 8.1 %collective-permute-start.34 = (bf16[1,1,1,1,1,64,768]{6,5,4,3,2,1,0:T(8,128)(2,1)S(1)}, bf16[1,1,1,1,1,64,768]{6,5,4,3,2,1,0:T(8,128)(2,1)S(1)}, u32[]{:S(2)}, u32[]{:S(2)}) collective-permute-start(bf16[1,1,1,1,1,64,768]{6,5,4,3,2,1,0:T(8,128)(2,1)S(1)} %add_convert_fusion.25), channel_id=1, source_target_pairs={{0,2},{1,3},{2,0},{3,1},{4,6},{5,7},{6,4},{7,5},{8,10},{9,11},{10,... | collective-permute-start | bytes 294920 | tf_op jit(solution)/shard_map/ppermute | solution.py:263
  313.2 15.8 %collective-permute-start.53 = (bf16[1,1,1,2,1,72,768]{6,5,4,3,2,1,0:T(8,128)(2,1)S(1)}, bf16[1,1,1,2,1,72,768]{6,5,4,3,2,1,0:T(8,128)(2,1)S(1)}, u32[]{:S(2)}, u32[]{:S(2)}) collective-permute-start(bf16[1,1,1,2,1,72,768]{6,5,4,3,2,1,0:T(8,128)(2,1)S(1)} %constant_dynamic-slice_fusion.1), channel_id=1, source_target_pairs={{0,16},{4,20},{8,24},{12,28},{16,0},{20,4},{24,8},{28,12},{1,17},{... | collective-permute-start | bytes 663560 | tf_op jit(solution)/shard_map/ppermute | solution.py:263
  320.3 45.0 %collective-permute-start.21 = (bf16[2,1,1,512,768]{4,3,2,1,0:T(8,128)(2,1)S(1)}, bf16[2,1,1,512,768]{4,3,2,1,0:T(8,128)(2,1)S(1)}, u32[]{:S(2)}, u32[]{:S(2)}) collective-permute-start(bf16[2,1,1,512,768]{4,3,2,1,0:T(8,128)(2,1)S(1)} %constant_dynamic-slice_fusion.25), channel_id=1, source_target_pairs={{0,2},{1,3},{2,0},{3,1},{4,6},{5,7},{6,4},{7,5},{8,10},{9,11},{10,... | collective-permute-start | bytes 4718600 | tf_op jit(solution)/shard_map/ppermute | solution.py:263
  320.6 8.8 %collective-permute-start.35 = (bf16[1,1,1,2,1,64,768]{6,5,4,3,2,1,0:T(8,128)(2,1)S(1)}, bf16[1,1,1,2,1,64,768]{6,5,4,3,2,1,0:T(8,128)(2,1)S(1)}, u32[]{:S(2)}, u32[]{:S(2)}) collective-permute-start(bf16[1,1,1,2,1,64,768]{6,5,4,3,2,1,0:T(8,128)(2,1)S(1)} %maximum_select_fusion.33), channel_id=1, source_target_pairs={{0,1},{1,0},{2,3},{3,2},{4,5},{5,4},{6,7},{7,6},{8,9},{9,8},{10,11... | collective-permute-start | bytes 589832 | tf_op jit(solution)/shard_map/ppermute | solution.py:263
  329.1 28.6 %collective-permute-start.54 = (bf16[1,1,1,1,1,72,768]{6,5,4,3,2,1,0:T(8,128)(2,1)S(1)}, bf16[1,1,1,1,1,72,768]{6,5,4,3,2,1,0:T(8,128)(2,1)S(1)}, u32[]{:S(2)}, u32[]{:S(2)}) collective-permute-start(bf16[1,1,1,1,1,72,768]{6,5,4,3,2,1,0:T(8,128)(2,1)S(1)} %constant_dynamic-slice_fusion), channel_id=1, source_target_pairs={{0,2},{1,3},{2,0},{3,1},{4,6},{5,7},{6,4},{7,5},{8,10},{9,11},{10,... | collective-permute-start | bytes 331784 | tf_op jit(solution)/shard_map/ppermute | solution.py:263
  375.4 25.5 %collective-permute-start.36 = (bf16[2,2,2,2,1,24,768]{6,5,4,3,2,1,0:T(8,128)(2,1)}, bf16[2,2,2,2,1,24,768]{6,5,4,3,2,1,0:T(8,128)(2,1)}, u32[]{:S(2)}, u32[]{:S(2)}) collective-permute-start(bf16[2,2,2,2,1,24,768]{6,5,4,3,2,1,0:T(8,128)(2,1)} %constant_dynamic-slice_fusion.14), channel_id=1, source_target_pairs={{0,1},{1,0},{2,3},{3,2},{4,5},{5,4},{6,7},{7,6},{8,9},{9,8},{10,11... | collective-permute-start | bytes 1769480 | tf_op jit(solution)/shard_map/ppermute | solution.py:263
  376.4 27.3 %collective-permute-start.43 = (bf16[2,2,2,2,1,24,768]{6,5,4,3,2,1,0:T(8,128)(2,1)}, bf16[2,2,2,2,1,24,768]{6,5,4,3,2,1,0:T(8,128)(2,1)}, u32[]{:S(2)}, u32[]{:S(2)}) collective-permute-start(bf16[2,2,2,2,1,24,768]{6,5,4,3,2,1,0:T(8,128)(2,1)} %constant_dynamic-slice_fusion.9), channel_id=1, source_target_pairs={{0,1},{1,0},{2,3},{3,2},{4,5},{5,4},{6,7},{7,6},{8,9},{9,8},{10,11... | collective-permute-start | bytes 1769480 | tf_op jit(solution)/shard_map/ppermute | solution.py:263
  397.5 8.1 %collective-permute-start.22 = (bf16[2,2,2,2,1,32,768]{6,5,4,3,2,1,0:T(8,128)(2,1)S(1)}, bf16[2,2,2,2,1,32,768]{6,5,4,3,2,1,0:T(8,128)(2,1)S(1)}, u32[]{:S(2)}, u32[]{:S(2)}) collective-permute-start(bf16[2,2,2,2,1,32,768]{6,5,4,3,2,1,0:T(8,128)(2,1)S(1)} %constant_dynamic-slice_fusion.24), channel_id=1, source_target_pairs={{0,1},{1,0},{2,3},{3,2},{4,5},{5,4},{6,7},{7,6},{8,9},{9,8},{10,11... | collective-permute-start | bytes 2359304 | tf_op jit(solution)/shard_map/ppermute | solution.py:263
  402.2 9.9 %collective-permute-start.37 = (bf16[2,2,1,2,1,24,768]{6,5,4,3,2,1,0:T(8,128)(2,1)S(1)}, bf16[2,2,1,2,1,24,768]{6,5,4,3,2,1,0:T(8,128)(2,1)S(1)}, u32[]{:S(2)}, u32[]{:S(2)}) collective-permute-start(bf16[2,2,1,2,1,24,768]{6,5,4,3,2,1,0:T(8,128)(2,1)S(1)} %constant_dynamic-slice_fusion.13), channel_id=1, source_target_pairs={{0,4},{4,0},{8,12},{12,8},{16,20},{20,16},{24,28},{28,24},{1,5},{5... | collective-permute-start | bytes 884744 | tf_op jit(solution)/shard_map/ppermute | solution.py:263
  405.0 12.7 %collective-permute-start.44 = (bf16[2,2,1,2,1,24,768]{6,5,4,3,2,1,0:T(8,128)(2,1)S(1)}, bf16[2,2,1,2,1,24,768]{6,5,4,3,2,1,0:T(8,128)(2,1)S(1)}, u32[]{:S(2)}, u32[]{:S(2)}) collective-permute-start(bf16[2,2,1,2,1,24,768]{6,5,4,3,2,1,0:T(8,128)(2,1)S(1)} %constant_dynamic-slice_fusion.8), channel_id=1, source_target_pairs={{0,4},{4,0},{8,12},{12,8},{16,20},{20,16},{24,28},{28,24},{1,5},{5... | collective-permute-start | bytes 884744 | tf_op jit(solution)/shard_map/ppermute | solution.py:263
  405.9 28.5 %collective-permute-start.23 = (bf16[2,2,2,1,1,32,768]{6,5,4,3,2,1,0:T(8,128)(2,1)S(1)}, bf16[2,2,2,1,1,32,768]{6,5,4,3,2,1,0:T(8,128)(2,1)S(1)}, u32[]{:S(2)}, u32[]{:S(2)}) collective-permute-start(bf16[2,2,2,1,1,32,768]{6,5,4,3,2,1,0:T(8,128)(2,1)S(1)} %constant_dynamic-slice_fusion.23), channel_id=1, source_target_pairs={{0,2},{1,3},{2,0},{3,1},{4,6},{5,7},{6,4},{7,5},{8,10},{9,11},{10,... | collective-permute-start | bytes 1179656 | tf_op jit(solution)/shard_map/ppermute | solution.py:263
  412.2 7.5 %collective-permute-start.38 = (bf16[2,2,1,1,1,24,768]{6,5,4,3,2,1,0:T(8,128)(2,1)S(1)}, bf16[2,2,1,1,1,24,768]{6,5,4,3,2,1,0:T(8,128)(2,1)S(1)}, u32[]{:S(2)}, u32[]{:S(2)}) collective-permute-start(bf16[2,2,1,1,1,24,768]{6,5,4,3,2,1,0:T(8,128)(2,1)S(1)} %constant_dynamic-slice_fusion.12), channel_id=1, source_target_pairs={{0,2},{1,3},{2,0},{3,1},{4,6},{5,7},{6,4},{7,5},{8,10},{9,11},{10,... | collective-permute-start | bytes 442376 | tf_op jit(solution)/shard_map/ppermute | solution.py:263
  417.7 5.4 %collective-permute-start.45 = (bf16[2,2,1,1,1,24,768]{6,5,4,3,2,1,0:T(8,128)(2,1)S(1)}, bf16[2,2,1,1,1,24,768]{6,5,4,3,2,1,0:T(8,128)(2,1)S(1)}, u32[]{:S(2)}, u32[]{:S(2)}) collective-permute-start(bf16[2,2,1,1,1,24,768]{6,5,4,3,2,1,0:T(8,128)(2,1)S(1)} %constant_dynamic-slice_fusion.7), channel_id=1, source_target_pairs={{0,2},{1,3},{2,0},{3,1},{4,6},{5,7},{6,4},{7,5},{8,10},{9,11},{10,... | collective-permute-start | bytes 442376 | tf_op jit(solution)/shard_map/ppermute | solution.py:263
  419.8 6.5 %collective-permute-start.39 = (bf16[2,1,1,1,1,24,768]{6,5,4,3,2,1,0:T(8,128)(2,1)S(1)}, bf16[2,1,1,1,1,24,768]{6,5,4,3,2,1,0:T(8,128)(2,1)S(1)}, u32[]{:S(2)}, u32[]{:S(2)}) collective-permute-start(bf16[2,1,1,1,1,24,768]{6,5,4,3,2,1,0:T(8,128)(2,1)S(1)} %constant_dynamic-slice_fusion.11), channel_id=1, source_target_pairs={{0,8},{4,12},{8,0},{12,4},{16,24},{20,28},{24,16},{28,20},{1,9},{5... | collective-permute-start | bytes 221192 | tf_op jit(solution)/shard_map/ppermute | solution.py:263
  423.2 5.8 %collective-permute-start.46 = (bf16[2,1,1,1,1,24,768]{6,5,4,3,2,1,0:T(8,128)(2,1)S(1)}, bf16[2,1,1,1,1,24,768]{6,5,4,3,2,1,0:T(8,128)(2,1)S(1)}, u32[]{:S(2)}, u32[]{:S(2)}) collective-permute-start(bf16[2,1,1,1,1,24,768]{6,5,4,3,2,1,0:T(8,128)(2,1)S(1)} %constant_dynamic-slice_fusion.6), channel_id=1, source_target_pairs={{0,8},{4,12},{8,0},{12,4},{16,24},{20,28},{24,16},{28,20},{1,9},{5... | collective-permute-start | bytes 221192 | tf_op jit(solution)/shard_map/ppermute | solution.py:263
  426.4 5.3 %collective-permute-start.40 = (bf16[1,1,1,1,1,24,768]{6,5,4,3,2,1,0:T(8,128)(2,1)S(1)}, bf16[1,1,1,1,1,24,768]{6,5,4,3,2,1,0:T(8,128)(2,1)S(1)}, u32[]{:S(2)}, u32[]{:S(2)}) collective-permute-start(bf16[1,1,1,1,1,24,768]{6,5,4,3,2,1,0:T(8,128)(2,1)S(1)} %constant_dynamic-slice_fusion.10), channel_id=1, source_target_pairs={{0,16},{4,20},{8,24},{12,28},{16,0},{20,4},{24,8},{28,12},{1,17},{... | collective-permute-start | bytes 110600 | tf_op jit(solution)/shard_map/ppermute | solution.py:263
  434.5 5.7 %collective-permute-start.24 = (bf16[2,2,1,1,1,32,768]{6,5,4,3,2,1,0:T(8,128)(2,1)S(1)}, bf16[2,2,1,1,1,32,768]{6,5,4,3,2,1,0:T(8,128)(2,1)S(1)}, u32[]{:S(2)}, u32[]{:S(2)}) collective-permute-start(bf16[2,2,1,1,1,32,768]{6,5,4,3,2,1,0:T(8,128)(2,1)S(1)} %constant_dynamic-slice_fusion.22), channel_id=1, source_target_pairs={{0,4},{4,0},{8,12},{12,8},{16,20},{20,16},{24,28},{28,24},{1,5},{5... | collective-permute-start | bytes 589832 | tf_op jit(solution)/shard_map/ppermute | solution.py:263
  435.8 6.2 %collective-permute-start.42 = (bf16[1,1,1,2,1,24,768]{6,5,4,3,2,1,0:T(8,128)(2,1)S(1)}, bf16[1,1,1,2,1,24,768]{6,5,4,3,2,1,0:T(8,128)(2,1)S(1)}, u32[]{:S(2)}, u32[]{:S(2)}) collective-permute-start(bf16[1,1,1,2,1,24,768]{6,5,4,3,2,1,0:T(8,128)(2,1)S(1)} %maximum_select_fusion.41), channel_id=1, source_target_pairs={{0,1},{1,0},{2,3},{3,2},{4,5},{5,4},{6,7},{7,6},{8,9},{9,8},{10,11... | collective-permute-start | bytes 221192 | tf_op jit(solution)/shard_map/ppermute | solution.py:263
  438.0 14.4 %collective-permute-start.49 = (bf16[1,1,1,2,1,24,768]{6,5,4,3,2,1,0:T(8,128)(2,1)S(1)}, bf16[1,1,1,2,1,24,768]{6,5,4,3,2,1,0:T(8,128)(2,1)S(1)}, u32[]{:S(2)}, u32[]{:S(2)}) collective-permute-start(bf16[1,1,1,2,1,24,768]{6,5,4,3,2,1,0:T(8,128)(2,1)S(1)} %maximum_select_fusion.42), channel_id=1, source_target_pairs={{0,1},{1,0},{2,3},{3,2},{4,5},{5,4},{6,7},{7,6},{8,9},{9,8},{10,11... | collective-permute-start | bytes 221192 | tf_op jit(solution)/shard_map/ppermute | solution.py:263
  (68 other events, 873.3 us)

commit v2 on v1

--- a/solution.py
+++ b/solution.py
@@ -300,27 +300,39 @@
     return gather(part, bits_down("dp") + ctx_used, order).reshape(-1, array.shape[1])
 
 
-def owned_sums(parts, order):
+def pack_parts(parts):
     ctx = lax.axis_size("ctx")
-    counts = [part.shape[1] for part in parts]
-    missing = -sum(counts) % (8 * ctx)
+    missing = -sum(part.shape[1] for part in parts) % (8 * ctx)
     if missing:
         last = jnp.pad(parts[-1], ((0, 0), (0, missing), (0, 0)))
         parts = parts[:-1] + [last]
     packed = jnp.concatenate(parts, 1) if len(parts) > 1 else parts[0]
-    total = packed.shape[1]
+    bits = len(bits_down("dp") + bits_down("ctx"))
+    return packed.reshape((2,) * bits + (packed.shape[1] // ctx, D))
+
+
+def halve_all(packed, order):
     places = bits_down("dp") + bits_down("ctx")
-    packed = packed.reshape((2,) * len(places) + (total // ctx, D))
     for step in order:
         packed = halve(packed, places.index(step), step)
+    return packed
+
+
+def unpack_sums(packed, counts):
+    places = bits_down("dp") + bits_down("ctx")
     for step in bits_down("ctx"):
         packed = double(packed, places.index(step), step)
-    full = packed.reshape(total, D).astype(jnp.float32)
+    full = packed.reshape(-1, D).astype(jnp.float32)
     found, start = [], 0
     for count in counts:
         found.append(full[start : start + count])
         start += count
     return found
+
+
+def owned_sums(parts, order):
+    counts = [part.shape[1] for part in parts]
+    return unpack_sums(halve_all(pack_parts(parts), order), counts)
 
 
 def by_owner(array):
@@ -416,19 +428,24 @@
     grad_down = contract(mixed_low, d_out_low, 0, 0)
     grad_in = [contract(normed_second, d_gate_up[:, i * D : (i + 1) * D], 0, 0) for i in range(3)]
     grad_out = contract(attended, d_branch, 0, 0)
-    in_sums = owned_sums(
-        [by_owner(part) for part in grad_in], core + near_x + along_z[::-1] + far
-    )
-    tail_sums = owned_sums(
-        [by_owner(grad_down), by_owner(grad_out), gain_row(grad_ffn_gain)],
-        core + far + near_x + along_z[::-1],
-    )
+    in_parts = [by_owner(part) for part in grad_in]
+    tail_parts = [by_owner(grad_down), by_owner(grad_out), gain_row(grad_ffn_gain)]
+    in_packed = halve_all(pack_parts(in_parts), core)
+    tail_packed = halve_all(pack_parts(tail_parts), core)
     d_att = contract(d_branch, out_full, 1, 1).astype(jnp.bfloat16)
+    d_att, in_packed, tail_packed = lax.optimization_barrier((d_att, in_packed, tail_packed))
+    in_packed = halve_all(in_packed, near_x)
+    tail_packed = halve_all(tail_packed, far)
     d_queries, d_kv_all = pull_attend(seen, queries, kv_all, d_att, attended_sum, log_total, marks)
     out_rows = mid_rows + jnp.dot(mixed_low, down_full, preferred_element_type=jnp.float32)
     d_kv = d_kv_all.reshape((2,) + (2,) * len(ctx_bits) + (rows_dev, D))
     for step in core + far:
         d_kv = halve(d_kv, 1 + ctx_bits.index(step), step)
+    d_kv, in_packed, tail_packed = lax.optimization_barrier((d_kv, in_packed, tail_packed))
+    in_packed = halve_all(in_packed, along_z[::-1] + far)
+    tail_packed = halve_all(tail_packed, near_x + along_z[::-1])
+    in_sums = unpack_sums(in_packed, [part.shape[1] for part in in_parts])
+    tail_sums = unpack_sums(tail_packed, [part.shape[1] for part in tail_parts])
     d_kv = d_kv.reshape(2, rows_dev, D)
     d_q = rotary(d_queries, cosine, -sine).astype(jnp.bfloat16)
     q_sums = owned_sums(

time: 464 us -> 454 us (0.978)
  waiting for transfers between devices: 161 us -> 142 us
  other arithmetic: 71.4 us -> 79.4 us
    ppermute x57, waiting for transfers between devices: 161 us -> 142 us  [swap(): return lax.ppermute(array, axis, [(i, i ^ bit) for i in range(count)])]
    convert_element_type x27, other arithmetic: 9.16 us -> 16.3 us  [halve(): (kept.astype(jnp.float32) + got.astype(jnp.float32)).astype(jnp.bfloat16)]
    unnamed x125 -> x119, local copies, waits for them, and re-layouts: 12.9 us -> 11.8 us
  transfers between devices with their start and end apart: 57 -> 57, of which waited for: 28 -> 27; matrix products, arithmetic and copies ran while one was open for 22% -> 25% of each run, Pallas kernels for 4% -> 0%
where the time goes in v2:
time: 454 us; the launch traced here: 446 us
  waiting for transfers between devices  142 us (31%)
  starting transfers between devices  98.6 us (22%)
  other arithmetic  79.4 us (17%)
  local copies, waits for them, and re-layouts  48.5 us (11%)
  matrix products  39.9 us (9%)
  Pallas kernels  35.8 us (8%)
    ppermute x57, waiting for transfers between devices, swap(): return lax.ppermute(array, axis, [(i, i ^ bit) for i in range(count)])  142 us
    ppermute x57, starting transfers between devices, swap(): return lax.ppermute(array, axis, [(i, i ^ bit) for i in range(count)])  98.6 us
    select_n x30, other arithmetic, double(): jnp.where(bit_here(step) == 0, jnp.concatenate([array, got], place), jnp....  33.3 us
    dot_general x13, matrix products, contract(): lax.dot_general(left, right, (((left_dim,), (right_dim,)), ((), ())), pre...  29.7 us
    pallas_call x1, Pallas kernels, pull_attend(): pl.pallas_call(pull_kernel, grid=(pairs,), in_specs=[pl.BlockSpec(memory_...  19.2 us
    pallas_call x1, Pallas kernels, attend(): pl.pallas_call(attend_kernel, grid=(pairs,), in_specs=[pl.BlockSpec(memor...  16.6 us
    convert_element_type x27, other arithmetic, halve(): (kept.astype(jnp.float32) + got.astype(jnp.float32)).astype(jnp.bfloat16)  16.3 us
    unnamed x119, local copies, waits for them, and re-layouts  11.8 us
  transfers between devices with their start and end apart: 57, of which 27 were waited for; matrix products, arithmetic and copies ran while one was open for 25% of the time, Pallas kernels for 0%

profile of v2, /device:TPU:0, one launch (start us, length us, event | category | flops | bytes accessed | tf_op | source)
XLA Modules:
  0.0 446.5 jit_solution(7404773918604337839)
XLA Ops:
  2.4 4.1 collective-permute-start
  9.5 2.9 collective-permute-start.12
  17.8 5.6 %collective-permute-done.5 = bf16[1,1,1,1,1,24,1536]{6,5,4,3,2,1,0:T(8,128)(2,1)S(1)} collective-permute-done((bf16[1,1,1,1,1,24,1536]{6,5,4,3,2,1,0:T(8,128)(2,1)S(1)}, bf16[1,1,1,1,1,24,1536]{6,5,4,3,2,1,0:T(8,128)(2,1)S(1)}, u32[]{:S(2)}, u32[]{:S(2)}) %collective-permute-start.5) | collective-permute-done | bytes 73760 | tf_op jit(solution)/shard_map/ppermute | solution.py:263
  25.2 7.8 %collective-permute-done.6 = bf16[2,1,1,1,1,24,1536]{6,5,0,4,3,2,1:T(8,128)(2,1)S(1)} collective-permute-done((bf16[2,1,1,1,1,24,1536]{6,5,0,4,3,2,1:T(8,128)(2,1)S(1)}, bf16[2,1,1,1,1,24,1536]{6,5,0,4,3,2,1:T(8,128)(2,1)S(1)}, u32[]{:S(2)}, u32[]{:S(2)}) %collective-permute-start.6) | collective-permute-done | bytes 147488 | tf_op jit(solution)/shard_map/ppermute | solution.py:263
  35.4 4.4 collective-permute-done.7
  45.7 2.4 tile.22
  51.7 2.5 maximum_select_fusion.11
  58.0 2.4 fusion.108
  61.0 3.1 maximum_select_fusion.4
  67.8 2.7 fusion.31
  79.2 5.8 %collective-permute-done.13 = bf16[2,1,1,1,120,768]{5,4,3,2,1,0:T(8,128)(2,1)S(1)} collective-permute-done((bf16[2,1,1,1,120,768]{5,4,3,2,1,0:T(8,128)(2,1)S(1)}, bf16[2,1,1,1,120,768]{5,4,3,2,1,0:T(8,128)(2,1)S(1)}, u32[]{:S(2)}, u32[]{:S(2)}) %collective-permute-start.13) | collective-permute-done | bytes 368672 | tf_op jit(solution)/shard_map/ppermute | solution.py:263
  86.8 6.4 %collective-permute-done.17 = bf16[2,1,1,1,48,2304]{5,4,3,2,1,0:T(8,128)(2,1)S(1)} collective-permute-done((bf16[2,1,1,1,48,2304]{5,4,3,2,1,0:T(8,128)(2,1)S(1)}, bf16[2,1,1,1,48,2304]{5,4,3,2,1,0:T(8,128)(2,1)S(1)}, u32[]{:S(2)}, u32[]{:S(2)}) %collective-permute-start.17) | collective-permute-done | bytes 442400 | tf_op jit(solution)/shard_map/ppermute | solution.py:263
  94.9 12.1 %collective-permute-done.10 = bf16[1,1,512,1536]{3,2,1,0:T(8,128)(2,1)} collective-permute-done((bf16[1,1,512,1536]{3,2,1,0:T(8,128)(2,1)S(1)}, bf16[1,1,512,1536]{3,2,1,0:T(8,128)(2,1)}, u32[]{:S(2)}, u32[]{:S(2)}) %collective-permute-start.10) | collective-permute-done | bytes 1572896 | tf_op jit(solution)/shard_map/ppermute | solution.py:263
  107.0 2.4 maximum_select_fusion.2
  111.5 8.7 %collective-permute-done.18 = bf16[2,2,1,1,48,2304]{5,4,3,2,1,0:T(8,128)(2,1)S(1)} collective-permute-done((bf16[2,2,1,1,48,2304]{5,4,3,2,1,0:T(8,128)(2,1)S(1)}, bf16[2,2,1,1,48,2304]{5,4,3,2,1,0:T(8,128)(2,1)S(1)}, u32[]{:S(2)}, u32[]{:S(2)}) %collective-permute-start.18) | collective-permute-done | bytes 884768 | tf_op jit(solution)/shard_map/ppermute | solution.py:263
  127.6 3.2 maximum_select_fusion.3
  131.1 5.4 %maximum_select_fusion.1 = bf16[2,2,2,2,48,2304]{5,4,3,2,1,0:T(8,128)(2,1)} fusion(bf16[2,2,2,1,48,2304]{5,4,3,2,1,0:T(8,128)(2,1)} %collective-permute-done.19, bf16[2,2,2,1,48,2304]{5,4,3,2,1,0:T(8,128)(2,1)} %maximum_select_fusion.5, pred[]{:T(512)S(6)} %eq.107), kind=kLoop, calls=%fused_computation.5 | loop fusion | flops 5308416 | bytes 7077889 | tf_op jit(solution)/shard_map/jit(_where)/select_n | solution.py:279
  136.6 6.8 %maximum_select_fusion = bf16[2,2,512,1536]{3,2,1,0:T(8,128)(2,1)} fusion(bf16[2,1,512,1536]{3,2,1,0:T(8,128)(2,1)} %collective-permute-done.11, bf16[2,1,512,1536]{3,2,1,0:T(8,128)(2,1)S(1)} %maximum_select_fusion.2, pred[]{:T(512)S(6)} %eq.107), kind=kLoop, calls=%fused_computation.2 | loop fusion | flops 9437184 | bytes 12582913 | tf_op jit(solution)/shard_map/jit(_where)/select_n | solution.py:279
  143.3 16.6 %shard_map.161 = (f32[512,768]{1,0:T(8,128)}, f32[6,2,512]{2,1,0:T(2,128)}) custom-call(s32[16]{0:T(128)} %reshape.3497.seen_ref, bf16[512,768]{1,0:T(8,128)(2,1)} %get-tuple-element.49.q_ref, bf16[2048,1536]{1,0:T(8,128)(2,1)} %bitcast.226, bf16[2048,1536]{1,0:T(8,128)(2,1)} %bitcast.227, s32[1,512]{1,0:T(1,128)} %bitcast.288, s32[1,512]{1,0:T(1,128)} %bitcast.284, ...), custom_call_target="tpu_custom_call" | custom-call | flops 3221225472 | bytes 12582912 | tf_op jit(solution)/shard_map/pallas_call | solution.py:165
  160.0 2.3 fusion.123
  166.3 6.1 %add_convert_fusion.4 = (bf16[512,1152]{1,0:T(8,128)(2,1)S(1)}, f32[512,1152]{1,0:T(8,128)S(1)}, f32[512,1152]{1,0:T(8,128)S(1)}) fusion(f32[512,2304]{1,0:T(8,128)S(1)} %fusion.124, bf16[1152,768]{1,0:T(8,128)(2,1)S(1)} %bitcast.259, bf16[1,512,768]{2,1,0:T(8,128)(2,1)S(1)} %copy-done.24), kind=kOutput, calls=%fused_computation.30 | convolution fusion | flops 949026816 | bytes 13172736 | tf_op jit(solution)/shard_map/dot_general | solution.py:25
  186.1 2.7 convolution_convert_fusion
  191.4 18.1 %collective-permute-start.21 = (bf16[2,2,2,2,1,64,768]{6,5,4,3,2,1,0:T(8,128)(2,1)}, bf16[2,2,2,2,1,64,768]{6,5,4,3,2,1,0:T(8,128)(2,1)}, u32[]{:S(2)}, u32[]{:S(2)}) collective-permute-start(bf16[2,2,2,2,1,64,768]{6,5,4,3,2,1,0:T(8,128)(2,1)} %constant_dynamic-slice_fusion.25), channel_id=1, source_target_pairs={{0,1},{1,0},{2,3},{3,2},{4,5},{5,4},{6,7},{7,6},{8,9},{9,8},{10,11... | collective-permute-start | bytes 4718600 | tf_op jit(solution)/shard_map/ppermute | solution.py:263
  213.3 3.3 convolution_convert_fusion.8.datt_ref
  216.7 3.2 add_convert_fusion.3
  219.9 3.2 add_convert_fusion.1
  223.1 19.2 %shard_map.162 = (f32[512,768]{1,0:T(8,128)}, bf16[2,2048,768]{2,1,0:T(8,128)(2,1)}) custom-call(s32[16]{0:T(128)} %reshape.3497.seen_ref, bf16[512,768]{1,0:T(8,128)(2,1)} %get-tuple-element.49.q_ref, bf16[2048,1536]{1,0:T(8,128)(2,1)} %bitcast.228, bf16[2048,1536]{1,0:T(8,128)(2,1)} %bitcast.229, bf16[512,768]{1,0:T(8,128)(2,1)} %convolution_convert_fusion.8.datt_ref, ...), custom_call_target="tpu_custom_call" | custom-call | flops 8053063680 | bytes 18874368 | tf_op jit(solution)/shard_map/pallas_call | solution.py:196
  242.3 3.8 constant_dynamic-slice_fusion.24
  246.1 21.3 %collective-permute-start.22 = (bf16[2,2,1,512,768]{4,3,2,1,0:T(8,128)(2,1)}, bf16[2,2,1,512,768]{4,3,2,1,0:T(8,128)(2,1)}, u32[]{:S(2)}, u32[]{:S(2)}) collective-permute-start(bf16[2,2,1,512,768]{4,3,2,1,0:T(8,128)(2,1)} %constant_dynamic-slice_fusion.24), channel_id=1, source_target_pairs={{0,1},{1,0},{2,3},{3,2},{4,5},{5,4},{6,7},{7,6},{8,9},{9,8},{10,11... | collective-permute-start | bytes 9437192 | tf_op jit(solution)/shard_map/ppermute | solution.py:263
  268.7 4.3 collective-permute-done.22
  273.0 3.6 add_convert_fusion
  282.5 6.6 %collective-permute-done.25 = bf16[2,2,2,1,1,64,768]{6,5,4,3,2,1,0:T(8,128)(2,1)S(1)} collective-permute-done((bf16[2,2,2,1,1,64,768]{6,5,4,3,2,1,0:T(8,128)(2,1)S(1)}, bf16[2,2,2,1,1,64,768]{6,5,4,3,2,1,0:T(8,128)(2,1)S(1)}, u32[]{:S(2)}, u32[]{:S(2)}) %collective-permute-start.25) | collective-permute-done | bytes 786464 | tf_op jit(solution)/shard_map/ppermute | solution.py:263
  290.2 10.0 %collective-permute-done.24 = bf16[2,2,1,2,1,72,768]{6,5,4,3,2,1,0:T(8,128)(2,1)S(1)} collective-permute-done((bf16[2,2,1,2,1,72,768]{6,5,4,3,2,1,0:T(8,128)(2,1)S(1)}, bf16[2,2,1,2,1,72,768]{6,5,4,3,2,1,0:T(8,128)(2,1)S(1)}, u32[]{:S(2)}, u32[]{:S(2)}) %collective-permute-start.24) | collective-permute-done | bytes 884768 | tf_op jit(solution)/shard_map/ppermute | solution.py:263
  300.3 21.5 %collective-permute-done.23 = bf16[2,1,1,512,768]{4,3,2,1,0:T(8,128)(2,1)S(1)} collective-permute-done((bf16[2,1,1,512,768]{4,3,2,1,0:T(8,128)(2,1)S(1)}, bf16[2,1,1,512,768]{4,3,2,1,0:T(8,128)(2,1)S(1)}, u32[]{:S(2)}, u32[]{:S(2)}) %collective-permute-start.23) | collective-permute-done | bytes 1572896 | tf_op jit(solution)/shard_map/ppermute | solution.py:263
  327.5 3.0 add_convert_fusion.9
  333.8 3.1 copy.89
  336.9 3.0 copy.90
  339.9 3.1 copy.88
  343.0 2.8 add_convert_fusion.7
  357.8 7.5 %collective-permute-done.33 = bf16[2,2,1,1,1,64,768]{6,5,4,3,2,1,0:T(8,128)(2,1)S(1)} collective-permute-done((bf16[2,2,1,1,1,64,768]{6,5,4,3,2,1,0:T(8,128)(2,1)S(1)}, bf16[2,2,1,1,1,64,768]{6,5,4,3,2,1,0:T(8,128)(2,1)S(1)}, u32[]{:S(2)}, u32[]{:S(2)}) %collective-permute-start.33) | collective-permute-done | bytes 393248 | tf_op jit(solution)/shard_map/ppermute | solution.py:263
  368.1 7.2 %collective-permute-start.53 = (bf16[1,1,1,2,1,72,768]{6,5,4,3,2,1,0:T(8,128)(2,1)S(1)}, bf16[1,1,1,2,1,72,768]{6,5,4,3,2,1,0:T(8,128)(2,1)S(1)}, u32[]{:S(2)}, u32[]{:S(2)}) collective-permute-start(bf16[1,1,1,2,1,72,768]{6,5,4,3,2,1,0:T(8,128)(2,1)S(1)} %constant_dynamic-slice_fusion.1), channel_id=1, source_target_pairs={{0,16},{4,20},{8,24},{12,28},{16,0},{20,4},{24,8},{28,12},{1,17},{... | collective-permute-start | bytes 663560 | tf_op jit(solution)/shard_map/ppermute | solution.py:263
  381.9 6.1 %collective-permute-done.53 = bf16[1,1,1,2,1,72,768]{6,5,4,3,2,1,0:T(8,128)(2,1)S(1)} collective-permute-done((bf16[1,1,1,2,1,72,768]{6,5,4,3,2,1,0:T(8,128)(2,1)S(1)}, bf16[1,1,1,2,1,72,768]{6,5,4,3,2,1,0:T(8,128)(2,1)S(1)}, u32[]{:S(2)}, u32[]{:S(2)}) %collective-permute-start.53) | collective-permute-done | bytes 221216 | tf_op jit(solution)/shard_map/ppermute | solution.py:263
  390.3 3.5 collective-permute-done.54
  402.2 8.4 %collective-permute-done.40 = bf16[2,2,1,1,1,24,768]{6,5,4,3,2,1,0:T(8,128)(2,1)S(1)} collective-permute-done((bf16[2,2,1,1,1,24,768]{6,5,4,3,2,1,0:T(8,128)(2,1)S(1)}, bf16[2,2,1,1,1,24,768]{6,5,4,3,2,1,0:T(8,128)(2,1)S(1)}, u32[]{:S(2)}, u32[]{:S(2)}) %collective-permute-start.40) | collective-permute-done | bytes 147488 | tf_op jit(solution)/shard_map/ppermute | solution.py:263
  426.4 2.8 collective-permute-done.28
  431.1 2.8 collective-permute-done.29
  435.5 3.6 collective-permute-done.30
  440.4 2.8 collective-permute-done.31
  (402 shorter events, 150.0 us)
Async XLA Ops:
  2.4 13.4 %collective-permute-start = (bf16[1,1,1,1,1,32,768]{6,5,4,3,2,1,0:T(8,128)(2,1)S(1)}, bf16[1,1,1,1,1,32,768]{6,5,4,3,2,1,0:T(8,128)(2,1)S(1)}, u32[]{:S(2)}, u32[]{:S(2)}) collective-permute-start(bf16[1,1,1,1,1,32,768]{6,5,4,3,2,1,0:T(8,128)(2,1)S(1)} %get-tuple-element.94), channel_id=1, source_target_pairs={{0,16},{4,20},{8,24},{12,28},{16,0},{20,4},{24,8},{28,12},{1,17},{... | collective-permute-start | bytes 147464 | tf_op jit(solution)/shard_map/ppermute | solution.py:263
  7.5 15.8 %collective-permute-start.5 = (bf16[1,1,1,1,1,24,1536]{6,5,4,3,2,1,0:T(8,128)(2,1)S(1)}, bf16[1,1,1,1,1,24,1536]{6,5,4,3,2,1,0:T(8,128)(2,1)S(1)}, u32[]{:S(2)}, u32[]{:S(2)}) collective-permute-start(bf16[1,1,1,1,1,24,1536]{6,5,4,3,2,1,0:T(8,128)(2,1)S(1)} %get-tuple-element.83), channel_id=1, source_target_pairs={{0,16},{4,20},{8,24},{12,28},{16,0},{20,4},{24,8},{28,12},{1,17},{... | collective-permute-start | bytes 221192 | tf_op jit(solution)/shard_map/ppermute | solution.py:263
  9.5 62.7 %collective-permute-start.12 = (bf16[1,1,1,1,120,768]{5,4,3,2,1,0:T(8,128)(2,1)}, bf16[1,1,1,1,120,768]{5,4,3,2,1,0:T(8,128)(2,1)}, u32[]{:S(2)}, u32[]{:S(2)}) collective-permute-start(bf16[1,1,1,1,120,768]{5,4,3,2,1,0:T(8,128)(2,1)} %get-tuple-element.79), channel_id=1, source_target_pairs={{0,16},{4,20},{8,24},{12,28},{16,0},{20,4},{24,8},{28,12},{1,17},{... | collective-permute-start | bytes 552968 | tf_op jit(solution)/shard_map/ppermute | solution.py:263
  13.2 61.5 %collective-permute-start.16 = (bf16[1,1,1,1,48,2304]{5,4,3,2,1,0:T(8,128)(2,1)}, bf16[1,1,1,1,48,2304]{5,4,3,2,1,0:T(8,128)(2,1)}, u32[]{:S(2)}, u32[]{:S(2)}) collective-permute-start(bf16[1,1,1,1,48,2304]{5,4,3,2,1,0:T(8,128)(2,1)} %get-tuple-element.75), channel_id=1, source_target_pairs={{0,16},{4,20},{8,24},{12,28},{16,0},{20,4},{24,8},{28,12},{1,17},{... | collective-permute-start | bytes 663560 | tf_op jit(solution)/shard_map/ppermute | solution.py:263
  15.9 7.6 %collective-permute-start.1 = (bf16[2,1,1,1,1,32,768]{6,5,4,3,2,1,0:T(8,128)(2,1)S(1)}, bf16[2,1,1,1,1,32,768]{6,5,4,3,2,1,0:T(8,128)(2,1)S(1)}, u32[]{:S(2)}, u32[]{:S(2)}) collective-permute-start(bf16[2,1,1,1,1,32,768]{6,5,4,3,2,1,0:T(8,128)(2,1)S(1)} %maximum_select_fusion.39), channel_id=1, source_target_pairs={{0,8},{4,12},{8,0},{12,4},{16,24},{20,28},{24,16},{28,20},{1,9},{5... | collective-permute-start | bytes 294920 | tf_op jit(solution)/shard_map/ppermute | solution.py:263
  23.4 9.6 %collective-permute-start.6 = (bf16[2,1,1,1,1,24,1536]{6,5,0,4,3,2,1:T(8,128)(2,1)S(1)}, bf16[2,1,1,1,1,24,1536]{6,5,0,4,3,2,1:T(8,128)(2,1)S(1)}, u32[]{:S(2)}, u32[]{:S(2)}) collective-permute-start(bf16[2,1,1,1,1,24,1536]{6,5,0,4,3,2,1:T(8,128)(2,1)S(1)} %fusion.64), channel_id=1, source_target_pairs={{0,8},{4,12},{8,0},{12,4},{16,24},{20,28},{24,16},{28,20},{1,9},{5... | collective-permute-start | bytes 442376 | tf_op jit(solution)/shard_map/ppermute | solution.py:263
  23.6 11.1 %collective-permute-start.2 = (bf16[2,2,1,1,1,32,768]{6,5,4,3,2,1,0:T(8,128)(2,1)S(1)}, bf16[2,2,1,1,1,32,768]{6,5,4,3,2,1,0:T(8,128)(2,1)S(1)}, u32[]{:S(2)}, u32[]{:S(2)}) collective-permute-start(bf16[2,2,1,1,1,32,768]{6,5,4,3,2,1,0:T(8,128)(2,1)S(1)} %maximum_select_fusion.31), channel_id=1, source_target_pairs={{0,2},{1,3},{2,0},{3,1},{4,6},{5,7},{6,4},{7,5},{8,10},{9,11},{10,... | collective-permute-start | bytes 589832 | tf_op jit(solution)/shard_map/ppermute | solution.py:263
  33.1 6.8 %collective-permute-start.7 = (bf16[2,2,1,1,1,24,1536]{6,5,4,3,2,1,0:T(8,128)(2,1)S(1)}, bf16[2,2,1,1,1,24,1536]{6,5,4,3,2,1,0:T(8,128)(2,1)S(1)}, u32[]{:S(2)}, u32[]{:S(2)}) collective-permute-start(bf16[2,2,1,1,1,24,1536]{6,5,4,3,2,1,0:T(8,128)(2,1)S(1)} %copy.73), channel_id=1, source_target_pairs={{0,4},{4,0},{8,12},{12,8},{16,20},{20,16},{24,28},{28,24},{1,5},{5... | collective-permute-start | bytes 884744 | tf_op jit(solution)/shard_map/ppermute | solution.py:263
  34.7 9.3 %collective-permute-start.3 = (bf16[2,2,1,2,1,32,768]{6,5,4,3,2,1,0:T(8,128)(2,1)S(1)}, bf16[2,2,1,2,1,32,768]{6,5,4,3,2,1,0:T(8,128)(2,1)S(1)}, u32[]{:S(2)}, u32[]{:S(2)}) collective-permute-start(bf16[2,2,1,2,1,32,768]{6,5,4,3,2,1,0:T(8,128)(2,1)S(1)} %maximum_select_fusion.23), channel_id=1, source_target_pairs={{0,4},{4,0},{8,12},{12,8},{16,20},{20,16},{24,28},{28,24},{1,5},{5... | collective-permute-start | bytes 1179656 | tf_op jit(solution)/shard_map/ppermute | solution.py:263
  40.8 10.9 %collective-permute-start.8 = (bf16[2,2,2,1,1,24,1536]{6,5,4,3,2,1,0:T(8,128)(2,1)}, bf16[2,2,2,1,1,24,1536]{6,5,4,3,2,1,0:T(8,128)(2,1)}, u32[]{:S(2)}, u32[]{:S(2)}) collective-permute-start(bf16[2,2,2,1,1,24,1536]{6,5,4,3,2,1,0:T(8,128)(2,1)} %maximum_select_fusion.18), channel_id=1, source_target_pairs={{0,2},{1,3},{2,0},{3,1},{4,6},{5,7},{6,4},{7,5},{8,10},{9,11},{10,... | collective-permute-start | bytes 1769480 | tf_op jit(solution)/shard_map/ppermute | solution.py:263
  45.0 9.6 %collective-permute-start.4 = (bf16[2,2,2,2,1,32,768]{6,5,4,3,2,1,0:T(8,128)(2,1)}, bf16[2,2,2,2,1,32,768]{6,5,4,3,2,1,0:T(8,128)(2,1)}, u32[]{:S(2)}, u32[]{:S(2)}) collective-permute-start(bf16[2,2,2,2,1,32,768]{6,5,4,3,2,1,0:T(8,128)(2,1)} %maximum_select_fusion.14), channel_id=1, source_target_pairs={{0,1},{1,0},{2,3},{3,2},{4,5},{5,4},{6,7},{7,6},{8,9},{9,8},{10,11... | collective-permute-start | bytes 2359304 | tf_op jit(solution)/shard_map/ppermute | solution.py:263
  54.1 6.9 %collective-permute-start.9 = (bf16[2,2,2,2,1,24,1536]{6,5,4,3,2,1,0:T(8,128)(2,1)}, bf16[2,2,2,2,1,24,1536]{6,5,4,3,2,1,0:T(8,128)(2,1)}, u32[]{:S(2)}, u32[]{:S(2)}) collective-permute-start(bf16[2,2,2,2,1,24,1536]{6,5,4,3,2,1,0:T(8,128)(2,1)} %maximum_select_fusion.11), channel_id=1, source_target_pairs={{0,1},{1,0},{2,3},{3,2},{4,5},{5,4},{6,7},{7,6},{8,9},{9,8},{10,11... | collective-permute-start | bytes 3538952 | tf_op jit(solution)/shard_map/ppermute | solution.py:263
  70.6 36.5 %collective-permute-start.10 = (bf16[1,1,512,1536]{3,2,1,0:T(8,128)(2,1)S(1)}, bf16[1,1,512,1536]{3,2,1,0:T(8,128)(2,1)}, u32[]{:S(2)}, u32[]{:S(2)}) collective-permute-start(bf16[1,1,512,1536]{3,2,1,0:T(8,128)(2,1)S(1)} %maximum_bitcast_fusion), channel_id=1, source_target_pairs={{0,2},{1,3},{2,0},{3,1},{4,6},{5,7},{6,4},{7,5},{8,10},{9,11},{10,... | collective-permute-start | bytes 4718600 | tf_op jit(solution)/shard_map/ppermute | solution.py:263
  73.5 11.6 %collective-permute-start.13 = (bf16[2,1,1,1,120,768]{5,4,3,2,1,0:T(8,128)(2,1)S(1)}, bf16[2,1,1,1,120,768]{5,4,3,2,1,0:T(8,128)(2,1)S(1)}, u32[]{:S(2)}, u32[]{:S(2)}) collective-permute-start(bf16[2,1,1,1,120,768]{5,4,3,2,1,0:T(8,128)(2,1)S(1)} %maximum_select_fusion.26), channel_id=1, source_target_pairs={{0,8},{4,12},{8,0},{12,4},{16,24},{20,28},{24,16},{28,20},{1,9},{5... | collective-permute-start | bytes 1105928 | tf_op jit(solution)/shard_map/ppermute | solution.py:263
  76.0 17.2 %collective-permute-start.17 = (bf16[2,1,1,1,48,2304]{5,4,3,2,1,0:T(8,128)(2,1)S(1)}, bf16[2,1,1,1,48,2304]{5,4,3,2,1,0:T(8,128)(2,1)S(1)}, u32[]{:S(2)}, u32[]{:S(2)}) collective-permute-start(bf16[2,1,1,1,48,2304]{5,4,3,2,1,0:T(8,128)(2,1)S(1)} %maximum_select_fusion.20), channel_id=1, source_target_pairs={{0,8},{4,12},{8,0},{12,4},{16,24},{20,28},{24,16},{28,20},{1,9},{5... | collective-permute-start | bytes 1327112 | tf_op jit(solution)/shard_map/ppermute | solution.py:263
  85.2 24.5 %collective-permute-start.14 = (bf16[2,2,1,1,120,768]{5,4,3,2,1,0:T(8,128)(2,1)S(1)}, bf16[2,2,1,1,120,768]{5,4,3,2,1,0:T(8,128)(2,1)S(1)}, u32[]{:S(2)}, u32[]{:S(2)}) collective-permute-start(bf16[2,2,1,1,120,768]{5,4,3,2,1,0:T(8,128)(2,1)S(1)} %maximum_select_fusion.16), channel_id=1, source_target_pairs={{0,4},{4,0},{8,12},{12,8},{16,20},{20,16},{24,28},{28,24},{1,5},{5... | collective-permute-start | bytes 2211848 | tf_op jit(solution)/shard_map/ppermute | solution.py:263
  93.4 26.8 %collective-permute-start.18 = (bf16[2,2,1,1,48,2304]{5,4,3,2,1,0:T(8,128)(2,1)S(1)}, bf16[2,2,1,1,48,2304]{5,4,3,2,1,0:T(8,128)(2,1)S(1)}, u32[]{:S(2)}, u32[]{:S(2)}) collective-permute-start(bf16[2,2,1,1,48,2304]{5,4,3,2,1,0:T(8,128)(2,1)S(1)} %maximum_select_fusion.13), channel_id=1, source_target_pairs={{0,4},{4,0},{8,12},{12,8},{16,20},{20,16},{24,28},{28,24},{1,5},{5... | collective-permute-start | bytes 2654216 | tf_op jit(solution)/shard_map/ppermute | solution.py:263
  109.4 27.2 %collective-permute-start.11 = (bf16[2,1,512,1536]{3,2,1,0:T(8,128)(2,1)S(1)}, bf16[2,1,512,1536]{3,2,1,0:T(8,128)(2,1)}, u32[]{:S(2)}, u32[]{:S(2)}) collective-permute-start(bf16[2,1,512,1536]{3,2,1,0:T(8,128)(2,1)S(1)} %maximum_select_fusion.2), channel_id=1, source_target_pairs={{0,1},{1,0},{2,3},{3,2},{4,5},{5,4},{6,7},{7,6},{8,9},{9,8},{10,11... | collective-permute-start | bytes 9437192 | tf_op jit(solution)/shard_map/ppermute | solution.py:263
  111.0 16.7 %collective-permute-start.15 = (bf16[2,2,2,1,120,768]{5,4,3,2,1,0:T(8,128)(2,1)}, bf16[2,2,2,1,120,768]{5,4,3,2,1,0:T(8,128)(2,1)}, u32[]{:S(2)}, u32[]{:S(2)}) collective-permute-start(bf16[2,2,2,1,120,768]{5,4,3,2,1,0:T(8,128)(2,1)} %maximum_select_fusion.10), channel_id=1, source_target_pairs={{0,1},{1,0},{2,3},{3,2},{4,5},{5,4},{6,7},{7,6},{8,9},{9,8},{10,11... | collective-permute-start | bytes 4423688 | tf_op jit(solution)/shard_map/ppermute | solution.py:263
  121.6 9.5 %collective-permute-start.19 = (bf16[2,2,2,1,48,2304]{5,4,3,2,1,0:T(8,128)(2,1)}, bf16[2,2,2,1,48,2304]{5,4,3,2,1,0:T(8,128)(2,1)}, u32[]{:S(2)}, u32[]{:S(2)}) collective-permute-start(bf16[2,2,2,1,48,2304]{5,4,3,2,1,0:T(8,128)(2,1)} %maximum_select_fusion.5), channel_id=1, source_target_pairs={{0,1},{1,0},{2,3},{3,2},{4,5},{5,4},{6,7},{7,6},{8,9},{9,8},{10,11... | collective-permute-start | bytes 5308424 | tf_op jit(solution)/shard_map/ppermute | solution.py:263
  191.4 25.2 %collective-permute-start.21 = (bf16[2,2,2,2,1,64,768]{6,5,4,3,2,1,0:T(8,128)(2,1)}, bf16[2,2,2,2,1,64,768]{6,5,4,3,2,1,0:T(8,128)(2,1)}, u32[]{:S(2)}, u32[]{:S(2)}) collective-permute-start(bf16[2,2,2,2,1,64,768]{6,5,4,3,2,1,0:T(8,128)(2,1)} %constant_dynamic-slice_fusion.25), channel_id=1, source_target_pairs={{0,1},{1,0},{2,3},{3,2},{4,5},{5,4},{6,7},{7,6},{8,9},{9,8},{10,11... | collective-permute-start | bytes 4718600 | tf_op jit(solution)/shard_map/ppermute | solution.py:263
  212.3 7.6 %collective-permute-start.20 = (bf16[2,2,2,2,1,72,768]{6,5,4,3,2,1,0:T(8,128)(2,1)}, bf16[2,2,2,2,1,72,768]{6,5,4,3,2,1,0:T(8,128)(2,1)}, u32[]{:S(2)}, u32[]{:S(2)}) collective-permute-start(bf16[2,2,2,2,1,72,768]{6,5,4,3,2,1,0:T(8,128)(2,1)} %constant_dynamic-slice_fusion.26), channel_id=1, source_target_pairs={{0,1},{1,0},{2,3},{3,2},{4,5},{5,4},{6,7},{7,6},{8,9},{9,8},{10,11... | collective-permute-start | bytes 5308424 | tf_op jit(solution)/shard_map/ppermute | solution.py:263
  246.1 26.9 %collective-permute-start.22 = (bf16[2,2,1,512,768]{4,3,2,1,0:T(8,128)(2,1)}, bf16[2,2,1,512,768]{4,3,2,1,0:T(8,128)(2,1)}, u32[]{:S(2)}, u32[]{:S(2)}) collective-permute-start(bf16[2,2,1,512,768]{4,3,2,1,0:T(8,128)(2,1)} %constant_dynamic-slice_fusion.24), channel_id=1, source_target_pairs={{0,1},{1,0},{2,3},{3,2},{4,5},{5,4},{6,7},{7,6},{8,9},{9,8},{10,11... | collective-permute-start | bytes 9437192 | tf_op jit(solution)/shard_map/ppermute | solution.py:263
  268.6 20.5 %collective-permute-start.25 = (bf16[2,2,2,1,1,64,768]{6,5,4,3,2,1,0:T(8,128)(2,1)S(1)}, bf16[2,2,2,1,1,64,768]{6,5,4,3,2,1,0:T(8,128)(2,1)S(1)}, u32[]{:S(2)}, u32[]{:S(2)}) collective-permute-start(bf16[2,2,2,1,1,64,768]{6,5,4,3,2,1,0:T(8,128)(2,1)S(1)} %constant_dynamic-slice_fusion.21), channel_id=1, source_target_pairs={{0,2},{1,3},{2,0},{3,1},{4,6},{5,7},{6,4},{7,5},{8,10},{9,11},{10,... | collective-permute-start | bytes 2359304 | tf_op jit(solution)/shard_map/ppermute | solution.py:263
  276.7 45.1 %collective-permute-start.23 = (bf16[2,1,1,512,768]{4,3,2,1,0:T(8,128)(2,1)S(1)}, bf16[2,1,1,512,768]{4,3,2,1,0:T(8,128)(2,1)S(1)}, u32[]{:S(2)}, u32[]{:S(2)}) collective-permute-start(bf16[2,1,1,512,768]{4,3,2,1,0:T(8,128)(2,1)S(1)} %constant_dynamic-slice_fusion.23), channel_id=1, source_target_pairs={{0,2},{1,3},{2,0},{3,1},{4,6},{5,7},{6,4},{7,5},{8,10},{9,11},{10,... | collective-permute-start | bytes 4718600 | tf_op jit(solution)/shard_map/ppermute | solution.py:263
  278.1 22.0 %collective-permute-start.24 = (bf16[2,2,1,2,1,72,768]{6,5,4,3,2,1,0:T(8,128)(2,1)S(1)}, bf16[2,2,1,2,1,72,768]{6,5,4,3,2,1,0:T(8,128)(2,1)S(1)}, u32[]{:S(2)}, u32[]{:S(2)}) collective-permute-start(bf16[2,2,1,2,1,72,768]{6,5,4,3,2,1,0:T(8,128)(2,1)S(1)} %constant_dynamic-slice_fusion.22), channel_id=1, source_target_pairs={{0,4},{4,0},{8,12},{12,8},{16,20},{20,16},{24,28},{28,24},{1,5},{5... | collective-permute-start | bytes 2654216 | tf_op jit(solution)/shard_map/ppermute | solution.py:263
  326.9 40.0 %collective-permute-start.52 = (bf16[2,1,1,2,1,72,768]{6,5,4,3,2,1,0:T(8,128)(2,1)}, bf16[2,1,1,2,1,72,768]{6,5,4,3,2,1,0:T(8,128)(2,1)}, u32[]{:S(2)}, u32[]{:S(2)}) collective-permute-start(bf16[2,1,1,2,1,72,768]{6,5,4,3,2,1,0:T(8,128)(2,1)} %constant_dynamic-slice_fusion.2), channel_id=1, source_target_pairs={{0,8},{4,12},{8,0},{12,4},{16,24},{20,28},{24,16},{28,20},{1,9},{5... | collective-permute-start | bytes 1327112 | tf_op jit(solution)/shard_map/ppermute | solution.py:263
  332.4 42.9 %collective-permute-start.38 = (bf16[2,2,2,2,1,24,768]{6,5,4,3,2,1,0:T(8,128)(2,1)}, bf16[2,2,2,2,1,24,768]{6,5,4,3,2,1,0:T(8,128)(2,1)}, u32[]{:S(2)}, u32[]{:S(2)}) collective-permute-start(bf16[2,2,2,2,1,24,768]{6,5,4,3,2,1,0:T(8,128)(2,1)} %constant_dynamic-slice_fusion.12), channel_id=1, source_target_pairs={{0,1},{1,0},{2,3},{3,2},{4,5},{5,4},{6,7},{7,6},{8,9},{9,8},{10,11... | collective-permute-start | bytes 1769480 | tf_op jit(solution)/shard_map/ppermute | solution.py:263
  333.3 45.0 %collective-permute-start.45 = (bf16[2,2,2,2,1,24,768]{6,5,4,3,2,1,0:T(8,128)(2,1)}, bf16[2,2,2,2,1,24,768]{6,5,4,3,2,1,0:T(8,128)(2,1)}, u32[]{:S(2)}, u32[]{:S(2)}) collective-permute-start(bf16[2,2,2,2,1,24,768]{6,5,4,3,2,1,0:T(8,128)(2,1)} %constant_dynamic-slice_fusion.7), channel_id=1, source_target_pairs={{0,1},{1,0},{2,3},{3,2},{4,5},{5,4},{6,7},{7,6},{8,9},{9,8},{10,11... | collective-permute-start | bytes 1769480 | tf_op jit(solution)/shard_map/ppermute | solution.py:263
  353.6 40.6 %collective-permute-start.26 = (bf16[2,2,2,2,1,32,768]{6,5,4,3,2,1,0:T(8,128)(2,1)S(1)}, bf16[2,2,2,2,1,32,768]{6,5,4,3,2,1,0:T(8,128)(2,1)S(1)}, u32[]{:S(2)}, u32[]{:S(2)}) collective-permute-start(bf16[2,2,2,2,1,32,768]{6,5,4,3,2,1,0:T(8,128)(2,1)S(1)} %constant_dynamic-slice_fusion.20), channel_id=1, source_target_pairs={{0,1},{1,0},{2,3},{3,2},{4,5},{5,4},{6,7},{7,6},{8,9},{9,8},{10,11... | collective-permute-start | bytes 2359304 | tf_op jit(solution)/shard_map/ppermute | solution.py:263
  353.7 11.6 %collective-permute-start.33 = (bf16[2,2,1,1,1,64,768]{6,5,4,3,2,1,0:T(8,128)(2,1)S(1)}, bf16[2,2,1,1,1,64,768]{6,5,4,3,2,1,0:T(8,128)(2,1)S(1)}, u32[]{:S(2)}, u32[]{:S(2)}) collective-permute-start(bf16[2,2,1,1,1,64,768]{6,5,4,3,2,1,0:T(8,128)(2,1)S(1)} %constant_dynamic-slice_fusion.15), channel_id=1, source_target_pairs={{0,4},{4,0},{8,12},{12,8},{16,20},{20,16},{24,28},{28,24},{1,5},{5... | collective-permute-start | bytes 1179656 | tf_op jit(solution)/shard_map/ppermute | solution.py:263
  365.4 14.5 %collective-permute-start.34 = (bf16[2,1,1,1,1,64,768]{6,5,4,3,2,1,0:T(8,128)(2,1)S(1)}, bf16[2,1,1,1,1,64,768]{6,5,4,3,2,1,0:T(8,128)(2,1)S(1)}, u32[]{:S(2)}, u32[]{:S(2)}) collective-permute-start(bf16[2,1,1,1,1,64,768]{6,5,4,3,2,1,0:T(8,128)(2,1)S(1)} %constant_dynamic-slice_fusion.14), channel_id=1, source_target_pairs={{0,8},{4,12},{8,0},{12,4},{16,24},{20,28},{24,16},{28,20},{1,9},{5... | collective-permute-start | bytes 589832 | tf_op jit(solution)/shard_map/ppermute | solution.py:263
  368.1 20.0 %collective-permute-start.53 = (bf16[1,1,1,2,1,72,768]{6,5,4,3,2,1,0:T(8,128)(2,1)S(1)}, bf16[1,1,1,2,1,72,768]{6,5,4,3,2,1,0:T(8,128)(2,1)S(1)}, u32[]{:S(2)}, u32[]{:S(2)}) collective-permute-start(bf16[1,1,1,2,1,72,768]{6,5,4,3,2,1,0:T(8,128)(2,1)S(1)} %constant_dynamic-slice_fusion.1), channel_id=1, source_target_pairs={{0,16},{4,20},{8,24},{12,28},{16,0},{20,4},{24,8},{28,12},{1,17},{... | collective-permute-start | bytes 663560 | tf_op jit(solution)/shard_map/ppermute | solution.py:263
  376.5 19.9 %collective-permute-start.39 = (bf16[2,2,1,2,1,24,768]{6,5,4,3,2,1,0:T(8,128)(2,1)S(1)}, bf16[2,2,1,2,1,24,768]{6,5,4,3,2,1,0:T(8,128)(2,1)S(1)}, u32[]{:S(2)}, u32[]{:S(2)}) collective-permute-start(bf16[2,2,1,2,1,24,768]{6,5,4,3,2,1,0:T(8,128)(2,1)S(1)} %constant_dynamic-slice_fusion.11), channel_id=1, source_target_pairs={{0,4},{4,0},{8,12},{12,8},{16,20},{20,16},{24,28},{28,24},{1,5},{5... | collective-permute-start | bytes 884744 | tf_op jit(solution)/shard_map/ppermute | solution.py:263
  379.6 17.3 %collective-permute-start.46 = (bf16[2,2,1,2,1,24,768]{6,5,4,3,2,1,0:T(8,128)(2,1)S(1)}, bf16[2,2,1,2,1,24,768]{6,5,4,3,2,1,0:T(8,128)(2,1)S(1)}, u32[]{:S(2)}, u32[]{:S(2)}) collective-permute-start(bf16[2,2,1,2,1,24,768]{6,5,4,3,2,1,0:T(8,128)(2,1)S(1)} %constant_dynamic-slice_fusion.6), channel_id=1, source_target_pairs={{0,4},{4,0},{8,12},{12,8},{16,20},{20,16},{24,28},{28,24},{1,5},{5... | collective-permute-start | bytes 884744 | tf_op jit(solution)/shard_map/ppermute | solution.py:263
  380.0 9.7 %collective-permute-start.35 = (bf16[1,1,1,1,1,64,768]{6,5,4,3,2,1,0:T(8,128)(2,1)S(1)}, bf16[1,1,1,1,1,64,768]{6,5,4,3,2,1,0:T(8,128)(2,1)S(1)}, u32[]{:S(2)}, u32[]{:S(2)}) collective-permute-start(bf16[1,1,1,1,1,64,768]{6,5,4,3,2,1,0:T(8,128)(2,1)S(1)} %constant_dynamic-slice_fusion.13), channel_id=1, source_target_pairs={{0,16},{4,20},{8,24},{12,28},{16,0},{20,4},{24,8},{28,12},{1,17},{... | collective-permute-start | bytes 294920 | tf_op jit(solution)/shard_map/ppermute | solution.py:263
  388.2 5.7 %collective-permute-start.54 = (bf16[1,1,1,1,1,72,768]{6,5,4,3,2,1,0:T(8,128)(2,1)S(1)}, bf16[1,1,1,1,1,72,768]{6,5,4,3,2,1,0:T(8,128)(2,1)S(1)}, u32[]{:S(2)}, u32[]{:S(2)}) collective-permute-start(bf16[1,1,1,1,1,72,768]{6,5,4,3,2,1,0:T(8,128)(2,1)S(1)} %constant_dynamic-slice_fusion), channel_id=1, source_target_pairs={{0,2},{1,3},{2,0},{3,1},{4,6},{5,7},{6,4},{7,5},{8,10},{9,11},{10,... | collective-permute-start | bytes 331784 | tf_op jit(solution)/shard_map/ppermute | solution.py:263
  389.8 6.6 %collective-permute-start.36 = (bf16[1,1,1,1,1,64,768]{6,5,4,3,2,1,0:T(8,128)(2,1)S(1)}, bf16[1,1,1,1,1,64,768]{6,5,4,3,2,1,0:T(8,128)(2,1)S(1)}, u32[]{:S(2)}, u32[]{:S(2)}) collective-permute-start(bf16[1,1,1,1,1,64,768]{6,5,4,3,2,1,0:T(8,128)(2,1)S(1)} %add_convert_fusion.25), channel_id=1, source_target_pairs={{0,2},{1,3},{2,0},{3,1},{4,6},{5,7},{6,4},{7,5},{8,10},{9,11},{10,... | collective-permute-start | bytes 294920 | tf_op jit(solution)/shard_map/ppermute | solution.py:263
  393.9 6.1 %collective-permute-start.55 = (bf16[1,1,1,1,1,72,768]{6,5,4,3,2,1,0:T(8,128)(2,1)S(1)}, bf16[1,1,1,1,1,72,768]{6,5,4,3,2,1,0:T(8,128)(2,1)S(1)}, u32[]{:S(2)}, u32[]{:S(2)}) collective-permute-start(bf16[1,1,1,1,1,72,768]{6,5,4,3,2,1,0:T(8,128)(2,1)S(1)} %add_convert_fusion.24), channel_id=1, source_target_pairs={{0,2},{1,3},{2,0},{3,1},{4,6},{5,7},{6,4},{7,5},{8,10},{9,11},{10,... | collective-permute-start | bytes 331784 | tf_op jit(solution)/shard_map/ppermute | solution.py:263
  394.5 28.8 %collective-permute-start.27 = (bf16[2,2,2,1,1,32,768]{6,5,4,3,2,1,0:T(8,128)(2,1)S(1)}, bf16[2,2,2,1,1,32,768]{6,5,4,3,2,1,0:T(8,128)(2,1)S(1)}, u32[]{:S(2)}, u32[]{:S(2)}) collective-permute-start(bf16[2,2,2,1,1,32,768]{6,5,4,3,2,1,0:T(8,128)(2,1)S(1)} %constant_dynamic-slice_fusion.19), channel_id=1, source_target_pairs={{0,2},{1,3},{2,0},{3,1},{4,6},{5,7},{6,4},{7,5},{8,10},{9,11},{10,... | collective-permute-start | bytes 1179656 | tf_op jit(solution)/shard_map/ppermute | solution.py:263
  396.5 14.1 %collective-permute-start.40 = (bf16[2,2,1,1,1,24,768]{6,5,4,3,2,1,0:T(8,128)(2,1)S(1)}, bf16[2,2,1,1,1,24,768]{6,5,4,3,2,1,0:T(8,128)(2,1)S(1)}, u32[]{:S(2)}, u32[]{:S(2)}) collective-permute-start(bf16[2,2,1,1,1,24,768]{6,5,4,3,2,1,0:T(8,128)(2,1)S(1)} %constant_dynamic-slice_fusion.10), channel_id=1, source_target_pairs={{0,2},{1,3},{2,0},{3,1},{4,6},{5,7},{6,4},{7,5},{8,10},{9,11},{10,... | collective-permute-start | bytes 442376 | tf_op jit(solution)/shard_map/ppermute | solution.py:263
  397.0 15.2 %collective-permute-start.47 = (bf16[2,2,1,1,1,24,768]{6,5,4,3,2,1,0:T(8,128)(2,1)S(1)}, bf16[2,2,1,1,1,24,768]{6,5,4,3,2,1,0:T(8,128)(2,1)S(1)}, u32[]{:S(2)}, u32[]{:S(2)}) collective-permute-start(bf16[2,2,1,1,1,24,768]{6,5,4,3,2,1,0:T(8,128)(2,1)S(1)} %constant_dynamic-slice_fusion.5), channel_id=1, source_target_pairs={{0,2},{1,3},{2,0},{3,1},{4,6},{5,7},{6,4},{7,5},{8,10},{9,11},{10,... | collective-permute-start | bytes 442376 | tf_op jit(solution)/shard_map/ppermute | solution.py:263
  400.0 12.9 %collective-permute-start.56 = (bf16[1,1,1,2,1,72,768]{6,5,4,3,2,1,0:T(8,128)(2,1)S(1)}, bf16[1,1,1,2,1,72,768]{6,5,4,3,2,1,0:T(8,128)(2,1)S(1)}, u32[]{:S(2)}, u32[]{:S(2)}) collective-permute-start(bf16[1,1,1,2,1,72,768]{6,5,4,3,2,1,0:T(8,128)(2,1)S(1)} %maximum_select_fusion.29), channel_id=1, source_target_pairs={{0,1},{1,0},{2,3},{3,2},{4,5},{5,4},{6,7},{7,6},{8,9},{9,8},{10,11... | collective-permute-start | bytes 663560 | tf_op jit(solution)/shard_map/ppermute | solution.py:263
  412.3 5.1 %collective-permute-start.48 = (bf16[2,1,1,1,1,24,768]{6,5,4,3,2,1,0:T(8,128)(2,1)S(1)}, bf16[2,1,1,1,1,24,768]{6,5,4,3,2,1,0:T(8,128)(2,1)S(1)}, u32[]{:S(2)}, u32[]{:S(2)}) collective-permute-start(bf16[2,1,1,1,1,24,768]{6,5,4,3,2,1,0:T(8,128)(2,1)S(1)} %constant_dynamic-slice_fusion.4), channel_id=1, source_target_pairs={{0,8},{4,12},{8,0},{12,4},{16,24},{20,28},{24,16},{28,20},{1,9},{5... | collective-permute-start | bytes 221192 | tf_op jit(solution)/shard_map/ppermute | solution.py:263
  415.1 5.5 %collective-permute-start.42 = (bf16[1,1,1,1,1,24,768]{6,5,4,3,2,1,0:T(8,128)(2,1)S(1)}, bf16[1,1,1,1,1,24,768]{6,5,4,3,2,1,0:T(8,128)(2,1)S(1)}, u32[]{:S(2)}, u32[]{:S(2)}) collective-permute-start(bf16[1,1,1,1,1,24,768]{6,5,4,3,2,1,0:T(8,128)(2,1)S(1)} %constant_dynamic-slice_fusion.8), channel_id=1, source_target_pairs={{0,16},{4,20},{8,24},{12,28},{16,0},{20,4},{24,8},{28,12},{1,17},{... | collective-permute-start | bytes 110600 | tf_op jit(solution)/shard_map/ppermute | solution.py:263
  423.5 5.7 %collective-permute-start.28 = (bf16[2,2,1,1,1,32,768]{6,5,4,3,2,1,0:T(8,128)(2,1)S(1)}, bf16[2,2,1,1,1,32,768]{6,5,4,3,2,1,0:T(8,128)(2,1)S(1)}, u32[]{:S(2)}, u32[]{:S(2)}) collective-permute-start(bf16[2,2,1,1,1,32,768]{6,5,4,3,2,1,0:T(8,128)(2,1)S(1)} %constant_dynamic-slice_fusion.18), channel_id=1, source_target_pairs={{0,4},{4,0},{8,12},{12,8},{16,20},{20,16},{24,28},{28,24},{1,5},{5... | collective-permute-start | bytes 589832 | tf_op jit(solution)/shard_map/ppermute | solution.py:263
  425.1 6.0 %collective-permute-start.44 = (bf16[1,1,1,2,1,24,768]{6,5,4,3,2,1,0:T(8,128)(2,1)S(1)}, bf16[1,1,1,2,1,24,768]{6,5,4,3,2,1,0:T(8,128)(2,1)S(1)}, u32[]{:S(2)}, u32[]{:S(2)}) collective-permute-start(bf16[1,1,1,2,1,24,768]{6,5,4,3,2,1,0:T(8,128)(2,1)S(1)} %maximum_select_fusion.41), channel_id=1, source_target_pairs={{0,1},{1,0},{2,3},{3,2},{4,5},{5,4},{6,7},{7,6},{8,9},{9,8},{10,11... | collective-permute-start | bytes 221192 | tf_op jit(solution)/shard_map/ppermute | solution.py:263
  426.3 14.1 %collective-permute-start.51 = (bf16[1,1,1,2,1,24,768]{6,5,4,3,2,1,0:T(8,128)(2,1)S(1)}, bf16[1,1,1,2,1,24,768]{6,5,4,3,2,1,0:T(8,128)(2,1)S(1)}, u32[]{:S(2)}, u32[]{:S(2)}) collective-permute-start(bf16[1,1,1,2,1,24,768]{6,5,4,3,2,1,0:T(8,128)(2,1)S(1)} %maximum_select_fusion.42), channel_id=1, source_target_pairs={{0,1},{1,0},{2,3},{3,2},{4,5},{5,4},{6,7},{7,6},{8,9},{9,8},{10,11... | collective-permute-start | bytes 221192 | tf_op jit(solution)/shard_map/ppermute | solution.py:263
  (65 other events, 459.7 us)
